TPU v7x, 128 devices: a whole 4x4x4 slice. The times are simulated.
128 devices in a mesh: seq: 32 (over y, z, core), head: 4 (over x).
Axes of the slice: x: 4, y: 4, z: 4, core: 2. Of those that a mesh axis runs over, the one named last changes fastest.
Arguments:
- queries: bfloat16 [16384, 32, 128], P('seq', 'head'), may hold values from -6 to 6
- key_vectors: bfloat16 [16384, 32, 128], P('seq', 'head'), may hold values from -6 to 6
- value_vectors: bfloat16 [16384, 32, 128], P('seq', 'head'), may hold values from -6 to 6
- doc_ids: int32 [16384], P('seq'), may hold values from 0 to 7, never falling along the last dimension, each value on 1 to 8192 neighbouring positions
- out_weight: bfloat16 [4096, 3072], P('head'), may hold values from -0.09375 to 0.09375
- grad_out: bfloat16 [16384, 3072], P('seq', 'head'), may hold values from -6 to 6
Outputs:
- layer_out: bfloat16 [16384, 3072], P('seq', 'head')
- grad_queries: bfloat16 [16384, 32, 128], P('seq', 'head')
- grad_keys: bfloat16 [16384, 32, 128], P('seq', 'head')
- grad_values: bfloat16 [16384, 32, 128], P('seq', 'head')
- grad_weight: float32 [4096, 3072], P('head', 'seq')
Inputs may be any that keep to these rules, and one draw needn't show every extreme that they name: doc_ids never falls; each of the 8 documents has 1 to 8192 tokens and one has exactly 8192.
All inputs are finite; a program needn't handle non-finite values.
Results may differ from a plain program's by a relative error of at most 0.0063.
Values may be sent and summed in bfloat16 or wider, within the bound.
No kernel may reach another device: no remote copies, remote signals or barrier semaphores. Data moves between devices by JAX's collectives and lax.ppermute only.
A program may use at most 128 MiB of HBM per device.

v0:
```python
import jax
import jax.numpy as jnp
from jax import lax
from jax.experimental import pallas as pl
from jax.experimental.pallas import tpu as pltpu
from jax.sharding import PartitionSpec as P

BF = jnp.bfloat16
F32 = jnp.float32
TOK, HEADS, DIM, FEAT, COLS = 512, 8, 128, 1024, 3072
HALF = HEADS // 2
ROWS = HALF * DIM
MIB = 2**20


def shape(dims, dtype):
    return jax.ShapeDtypeStruct(dims, dtype)


def whole():
    return pl.BlockSpec(memory_space=pltpu.VMEM)


def scalars():
    return pl.BlockSpec(memory_space=pltpu.SMEM)


def params(mib):
    return pltpu.CompilerParams(vmem_limit_bytes=mib * MIB)


def cost(flops, moved):
    return pl.CostEstimate(flops=flops, bytes_accessed=moved, transcendentals=0)


def dot(a, b, ca, cb):
    return lax.dot_general(a, b, (((ca,), (cb,)), ((), ())), preferred_element_type=F32)


def fixed(*dims):
    return pl.BlockSpec(dims, lambda n: (0,) * len(dims))


def in_hbm():
    return pl.BlockSpec(memory_space=pltpu.HBM)


def anywhere():
    return pl.BlockSpec(memory_space=pl.ANY)


def upright(docs_row, width):
    docs_row = docs_row.astype(F32)
    return jnp.broadcast_to(docs_row, (width, docs_row.shape[1])).T


def prepare_kernel(place, q_hbm, k_hbm, v_hbm, docs_hbm, cot_hbm, qh_ref, kh_ref, vh_ref, keep_ref, give_ref, cot_ref, q_buf, k_buf, v_buf, docs_buf, own, sems, docs_sem, cot_sem):
    steps = k_buf.shape[0]
    rows = TOK // steps

    def fetch(n, source, target, sem):
        copy = pltpu.make_async_copy(source.at[n * rows : (n + 1) * rows], target.at[n], sem)
        copy.start()
        return copy

    docs_copy = pltpu.make_async_copy(docs_hbm, docs_buf, docs_sem)
    docs_copy.start()
    copies = []
    for n in range(steps):
        copies.append(fetch(n, k_hbm, k_buf, sems.at[0, n]))
        copies.append(fetch(n, v_hbm, v_buf, sems.at[1, n]))
    q_copies = [fetch(n, q_hbm, q_buf, sems.at[2, n]) for n in range(steps)]
    cot_copy = pltpu.make_async_copy(cot_hbm, cot_ref, cot_sem)
    cot_copy.start()
    c = place[2]
    docs_copy.wait()
    docs = docs_buf[...].astype(F32)
    last = docs[:, TOK - 1 :]
    tail = (upright(docs, DIM) == last).astype(BF)
    for n in range(steps):
        span = slice(n * rows, (n + 1) * rows)
        copies[2 * n].wait()
        copies[2 * n + 1].wait()
        kh = jnp.swapaxes(k_buf[n], 0, 1)
        vh = jnp.swapaxes(v_buf[n], 0, 1)
        kh_ref[:, span] = kh
        vh_ref[:, span] = vh
        for h in range(HEADS):
            part = dot(kh[h] * tail[span], vh[h], 0, 0)
            spot = slice((h % HALF) * DIM, (h % HALF + 1) * DIM)
            if n == 0:
                own[h // HALF, spot] = part
            else:
                own[h // HALF, spot] += part
    keep_ref[:ROWS] = own[c]
    give_ref[:ROWS] = own[1 - c]
    doc_rows = jnp.broadcast_to(last, (8, DIM))
    keep_ref[ROWS:] = doc_rows
    give_ref[ROWS:] = doc_rows
    for n in range(steps):
        q_copies[n].wait()
        qh_ref[:, n * rows : (n + 1) * rows] = jnp.swapaxes(q_buf[n], 0, 1)
    cot_copy.wait()


def prepare(place, queries, keys, values, docs, cotangent):
    steps = 2
    head_major = shape((HEADS, TOK, DIM), BF)
    half = shape((ROWS + 8, DIM), F32)
    buffer = pltpu.VMEM((steps, TOK // steps, HEADS, DIM), BF)
    return pl.pallas_call(
        prepare_kernel,
        out_shape=(head_major, head_major, head_major, half, half, shape((TOK, 768), BF)),
        in_specs=[scalars()] + [in_hbm()] * 5,
        out_specs=(whole(),) * 6,
        scratch_shapes=[
            buffer,
            buffer,
            buffer,
            pltpu.VMEM((1, TOK), jnp.int32),
            pltpu.VMEM((2, ROWS, DIM), F32),
            pltpu.SemaphoreType.DMA((3, steps)),
            pltpu.SemaphoreType.DMA,
            pltpu.SemaphoreType.DMA,
        ],
        compiler_params=params(12),
        cost_estimate=cost(2 * HEADS * TOK * DIM * DIM, 6 * MIB),
        name="prepare",
    )(place, *[pltpu.with_memory_space_constraint(a, pltpu.HBM) for a in (queries, keys, values, docs, cotangent)])


def chip_kernel(forward, place, keep_ref, got_ref, *rest):
    far_ref, chip_ref = rest[-2:]
    c = place[2]
    far_is_mine = (c == 0) if forward else (c == 1)

    def write(far, near):
        same = (far[ROWS : ROWS + 1] == near[ROWS : ROWS + 1]).astype(F32)
        far_ref[...] = far[...]
        chip_ref[:ROWS] = (near[:ROWS] + same * far[:ROWS]).astype(BF)
        chip_ref[ROWS:] = jnp.broadcast_to(near[ROWS : ROWS + 1], (16, DIM)).astype(BF)

    @pl.when(far_is_mine)
    def _():
        write(keep_ref, got_ref)

    @pl.when(jnp.logical_not(far_is_mine))
    def _():
        write(got_ref, keep_ref)


def chip_state(place, keep, got, forward, *earlier):
    def kernel(*refs):
        chip_kernel(forward, *refs)

    return pl.pallas_call(
        kernel,
        out_shape=(shape((ROWS + 8, DIM), F32), shape((ROWS + 16, DIM), BF)),
        in_specs=[scalars(), whole(), whole()] + [anywhere()] * len(earlier),
        out_specs=(whole(), whole()),
        compiler_params=params(4),
        cost_estimate=cost(ROWS * DIM * 3, MIB),
        name="chip_state",
    )(place, keep, got, *earlier)


def spot_of(place, forward, step):
    chip = place[0] * 4 + place[1]
    spot = lax.rem(chip // step, 2)
    return spot if forward else 1 - spot


def join_kernel(forward, step, place, own_ref, other_ref, *rest):
    out_ref = rest[-1]
    first = spot_of(place, forward, step) == 0

    def write(early, late):
        doc = late[ROWS : ROWS + 1]
        same = (early[ROWS : ROWS + 1] == doc).astype(F32)
        total = late[:ROWS].astype(F32) + same * early[:ROWS].astype(F32)
        out_ref[:ROWS] = total.astype(BF)
        out_ref[ROWS:] = jnp.broadcast_to(doc, (16, DIM))

    @pl.when(first)
    def _():
        write(own_ref, other_ref)

    @pl.when(jnp.logical_not(first))
    def _():
        write(other_ref, own_ref)


def join(place, own, other, forward, step, *earlier):
    def kernel(*refs):
        join_kernel(forward, step, *refs)

    return pl.pallas_call(
        kernel,
        out_shape=shape((ROWS + 16, DIM), BF),
        in_specs=[scalars()] + [whole()] * 2 + [anywhere()] * len(earlier),
        out_specs=whole(),
        compiler_params=params(4),
        cost_estimate=cost(ROWS * DIM * 3, MIB),
        name="join",
    )(place, own, other, *earlier)


def entry_kernel(forward, steps, place, far_ref, *refs):
    parts, (keep_ref, give_ref, doc_ref) = refs[: len(steps)], refs[-3:]
    y, c = place[0], place[2]
    level = y if forward else 3 - y
    far_is_mine = (c == 0) if forward else (c == 1)
    inside = [spot_of(place, forward, step) == 1 if step > 0 else level >= -step for step in steps]
    docs = [p[ROWS : ROWS + 1].astype(F32) for p in parts]
    before_doc = jnp.full((1, DIM), -1.0, F32)
    for k in reversed(range(len(steps))):
        before_doc = jnp.where(inside[k], docs[k], before_doc)
    before = jnp.zeros((ROWS, DIM), F32)
    for k in range(len(steps)):
        use = jnp.where(inside[k], (docs[k] == before_doc).astype(F32), 0.0)
        before = before + use * parts[k][:ROWS].astype(F32)
    far_doc = far_ref[ROWS : ROWS + 1]
    after = far_ref[:ROWS] + (before_doc == far_doc).astype(F32) * before

    @pl.when(far_is_mine)
    def _():
        keep_ref[...] = before.astype(BF)
        give_ref[...] = after.astype(BF)
        doc_ref[...] = jnp.broadcast_to(before_doc, (8, DIM))

    @pl.when(jnp.logical_not(far_is_mine))
    def _():
        keep_ref[...] = after.astype(BF)
        give_ref[...] = before.astype(BF)
        doc_ref[...] = jnp.broadcast_to(far_doc, (8, DIM))


def entry_state(place, far, parts, steps, forward, *earlier):
    def kernel(*refs):
        entry_kernel(forward, steps, *refs)

    half = shape((ROWS, DIM), BF)
    return pl.pallas_call(
        kernel,
        out_shape=(half, half, shape((8, DIM), F32)),
        in_specs=[scalars()] + [whole()] * (1 + len(parts)) + [anywhere()] * len(earlier),
        out_specs=(whole(),) * 3,
        compiler_params=params(4),
        cost_estimate=cost(ROWS * DIM * 10, MIB),
        name="entry_state",
    )(place, far, *parts, *earlier)


def causal(docs_ref):
    row = jnp.broadcast_to(docs_ref[...].astype(F32), (TOK, TOK))
    t = lax.broadcasted_iota(jnp.int32, (TOK, TOK), 0)
    s = lax.broadcasted_iota(jnp.int32, (TOK, TOK), 1)
    same = row.T == row
    return (t >= s) & same, (s >= t) & same


def intra_kernel(q_ref, k_ref, v_ref, docs_ref, *rest):
    attn_ref, mask = rest[-2:]
    mask[...] = causal(docs_ref)[0].astype(BF)
    mid = TOK // 2
    for h in range(q_ref.shape[0]):
        for rows, width in ((slice(0, mid), mid), (slice(mid, TOK), TOK)):
            scores = dot(q_ref[h, rows], k_ref[h, :width], 1, 1).astype(BF) * mask[rows, :width]
            attn_ref[h, rows] = dot(scores, v_ref[h, :width], 1, 0)


def intra(qh, kh, vh, docs, group, *earlier):
    part = pl.BlockSpec((HALF, TOK, DIM), lambda n: (group, 0, 0))
    return pl.pallas_call(
        intra_kernel,
        grid=(1,),
        out_shape=shape((HALF, TOK, DIM), F32),
        in_specs=[part, part, part, fixed(1, TOK)] + [anywhere()] * len(earlier),
        out_specs=fixed(HALF, TOK, DIM),
        scratch_shapes=[pltpu.VMEM((TOK, TOK), BF)],
        compiler_params=params(14),
        cost_estimate=cost(2 * HEADS * TOK * TOK * DIM, 3 * MIB),
        name="intra",
    )(qh, kh, vh, docs, *earlier)


def upper_kernel(q_ref, k_ref, docs_ref, *rest):
    out_ref, mask = rest[-2:]
    mask[...] = causal(docs_ref)[1].astype(BF)
    mid = TOK // 2
    for h in range(HEADS):
        for rows, start in ((slice(0, mid), 0), (slice(mid, TOK), mid)):
            scores = dot(k_ref[h, rows], q_ref[h, start:], 1, 1)
            out_ref[h, rows, start:] = scores.astype(BF) * mask[rows, start:]


def upper_scores(qh, kh, docs, *earlier):
    return pl.pallas_call(
        upper_kernel,
        out_shape=shape((HEADS, TOK, TOK), BF),
        in_specs=[whole()] * 3 + [anywhere()] * len(earlier),
        out_specs=whole(),
        scratch_shapes=[pltpu.VMEM((TOK, TOK), BF)],
        compiler_params=params(10),
        cost_estimate=cost(2 * HEADS * TOK * TOK * DIM, 6 * MIB),
        name="upper_scores",
    )(qh, kh, docs, *earlier)


def pick_state(c, keep_ref, take_ref, h):
    rows = slice((h % HALF) * DIM, (h % HALF + 1) * DIM)
    mine = c == h // HALF
    return jnp.where(mine, keep_ref[rows], take_ref[rows])


def attend_kernel(place, q_ref, intra0, intra1, keep_ref, take_ref, doc_ref, docs_ref, *rest):
    attn_ref, normed_ref = rest[-2:]
    c = place[2]
    reads = (upright(docs_ref[...], DIM) == doc_ref[:1]).astype(F32)
    for h in range(HEADS):
        state = pick_state(c, keep_ref, take_ref, h)
        attn = (intra0, intra1)[h // HALF][h % HALF] + reads * dot(q_ref[h], state, 1, 0)
        attn_ref[h] = attn
        scale = lax.rsqrt(jnp.mean(attn * attn, axis=-1, keepdims=True) + 1e-05)
        normed_ref[:, h * DIM : (h + 1) * DIM] = (attn * scale).astype(BF)


def attend(place, qh, intra0, intra1, keep, take, doc, docs, *earlier):
    return pl.pallas_call(
        attend_kernel,
        out_shape=(shape((HEADS, TOK, DIM), F32), shape((TOK, FEAT), BF)),
        in_specs=[scalars()] + [whole()] * 7 + [anywhere()] * len(earlier),
        out_specs=(whole(), whole()),
        compiler_params=params(8),
        cost_estimate=cost(2 * HEADS * TOK * DIM * DIM, 6 * MIB),
        name="attend",
    )(place, qh, intra0, intra1, keep, take, doc, docs, *earlier)


def project_kernel(places, place, normed_ref, w_hbm, *rest):
    outs, (w_buf, sems) = rest[-3 - len(places) : -2], rest[-2:]
    x = place[3]
    copies = []
    for n, r in enumerate(places):
        spot = pl.multiple_of(lax.rem(x + r, 4) * 768, 768)
        copies.append(pltpu.make_async_copy(w_hbm.at[:, pl.ds(spot, 768)], w_buf.at[n], sems.at[n]))
        copies[n].start()
    for n, r in enumerate(places):
        copies[n].wait()
        part = jnp.dot(normed_ref[...], w_buf[n], preferred_element_type=F32)
        if r == 2:
            mid = TOK // 2
            outs[0][...] = part[:mid].astype(BF)
            outs[1][...] = part[mid:].astype(BF)
        else:
            outs[n + 1][...] = part.astype(outs[n + 1].dtype)


def project(place, places, normed, weight, *earlier):
    outs = []
    for r in places:
        if r == 2:
            outs += [shape((TOK // 2, 768), BF)] * 2
        else:
            outs.append(shape((TOK, 768), BF if r else F32))
    shift = 0 if 2 in places else 1

    def kernel(*refs):
        ahead = 3 + len(earlier)
        project_kernel(places, *refs[:ahead], *([None] * shift), *refs[ahead:])

    return pl.pallas_call(
        kernel,
        out_shape=tuple(outs),
        in_specs=[scalars(), whole(), in_hbm()] + [anywhere()] * len(earlier),
        out_specs=(whole(),) * len(outs),
        scratch_shapes=[pltpu.VMEM((len(places), FEAT, 768), BF), pltpu.SemaphoreType.DMA((len(places),))],
        compiler_params=params(4 + 3 * len(places)),
        cost_estimate=cost(TOK * FEAT * COLS * len(places) // 2, 3 * MIB * len(places)),
        name="project",
    )(place, normed, weight, *earlier)


def halves_kernel(left_ref, right_ref, *rest):
    top_ref, bottom_ref = rest[-2:]
    mid = TOK // 2
    top_ref[...] = left_ref[:mid]
    bottom_ref[...] = right_ref[mid:]


def halves(left, right, *earlier):
    out = shape((TOK // 2, 768), BF)
    return pl.pallas_call(
        halves_kernel,
        out_shape=(out, out),
        in_specs=[whole()] * 2 + [anywhere()] * len(earlier),
        out_specs=(whole(),) * 2,
        compiler_params=params(6),
        cost_estimate=cost(TOK * 768, 2 * MIB),
        name="halves",
    )(left, right, *earlier)


def out_pass_kernel(right_ref, left_ref, top_ref, bottom_ref, *rest):
    out_right, out_left = rest[-2:]
    mid = TOK // 2
    out_right[:mid] = (right_ref[:mid].astype(F32) + top_ref[...].astype(F32)).astype(BF)
    out_right[mid:] = right_ref[mid:]
    out_left[:mid] = left_ref[:mid]
    out_left[mid:] = (left_ref[mid:].astype(F32) + bottom_ref[...].astype(F32)).astype(BF)


def out_pass(right, left, top, bottom, *earlier):
    part = shape((TOK, 768), BF)
    return pl.pallas_call(
        out_pass_kernel,
        out_shape=(part, part),
        in_specs=[whole()] * 4 + [anywhere()] * len(earlier),
        out_specs=(whole(), whole()),
        compiler_params=params(6),
        cost_estimate=cost(TOK * 768, 4 * MIB),
        name="out_pass",
    )(right, left, top, bottom, *earlier)


def out_end_kernel(own_ref, left_ref, right_ref, *rest):
    total = own_ref[...] + left_ref[...].astype(F32) + right_ref[...].astype(F32)
    rest[-1][...] = total.astype(BF)


def out_end(own, from_left, from_right, *earlier):
    return pl.pallas_call(
        out_end_kernel,
        out_shape=shape((TOK, 768), BF),
        in_specs=[whole()] * 3 + [anywhere()] * len(earlier),
        out_specs=whole(),
        compiler_params=params(6),
        cost_estimate=cost(2 * TOK * 768, 4 * MIB),
        name="out_end",
    )(own, from_left, from_right, *earlier)


def turn_kernel(place, own_ref, right_ref, top_ref, bottom_ref, left_ref, *rest):
    joined_ref, keep_ref, give_ref = rest[-3:]
    c, x = place[2], place[3]
    mid = TOK // 2
    for r, ref, tokens in (
        (0, own_ref, slice(0, TOK)),
        (1, right_ref, slice(0, TOK)),
        (3, left_ref, slice(0, TOK)),
        (2, top_ref, slice(0, mid)),
        (2, bottom_ref, slice(mid, TOK)),
    ):
        block = ref[...]
        spot = pl.multiple_of(lax.rem(x + r, 4) * 768, 768)
        joined_ref[tokens, pl.ds(spot, 768)] = block
        turned = block.T.reshape(4, 2, 96, block.shape[0])
        low, high = turned[:, 0], turned[:, 1]
        keep_ref[r, :, :, tokens] = jnp.where(c == 0, low, high)
        give_ref[r, :, :, tokens] = jnp.where(c == 0, high, low)


def turn(place, own, right, top, bottom, left, *earlier):
    out = shape((4, 4, 96, TOK), BF)
    return pl.pallas_call(
        turn_kernel,
        out_shape=(shape((TOK, COLS), BF), out, out),
        in_specs=[scalars()] + [whole()] * 5 + [anywhere()] * len(earlier),
        out_specs=(whole(),) * 3,
        compiler_params=params(8),
        cost_estimate=cost(TOK * COLS, 6 * MIB),
        name="turn",
    )(place, own, right, top, bottom, left, *earlier)


def back_kernel(place, cot_ref, w_ref, attn_ref, q_ref, docs_ref, *rest):
    grad_ref, keep_ref, give_ref, own = rest[-4:]
    c = place[2]
    pairs = HEADS // 2
    docs = docs_ref[...].astype(F32)
    first = docs[:, :1]
    lead = (upright(docs, DIM) == first).astype(BF)
    for n in range(pairs):
        grad_normed = dot(cot_ref[...], w_ref[n * 2 * DIM : (n + 1) * 2 * DIM], 1, 1)
        for j in range(2):
            h = 2 * n + j
            attn = attn_ref[h]
            scale = lax.rsqrt(jnp.mean(attn * attn, axis=-1, keepdims=True) + 1e-05)
            normed = attn * scale
            grad = grad_normed[:, j * DIM : (j + 1) * DIM]
            grad = scale * (grad - normed * jnp.mean(grad * normed, axis=-1, keepdims=True))
            grad = grad.astype(BF)
            grad_ref[h] = grad
            spot = slice((h % HALF) * DIM, (h % HALF + 1) * DIM)
            own[h // HALF, spot] = dot(q_ref[h] * lead, grad, 0, 0)
    keep_ref[:ROWS] = own[c]
    give_ref[:ROWS] = own[1 - c]
    doc_rows = jnp.broadcast_to(first, (8, DIM))
    keep_ref[ROWS:] = doc_rows
    give_ref[ROWS:] = doc_rows


def back(place, cotangent, weight, attn, qh, docs, *earlier):
    half = shape((ROWS + 8, DIM), F32)
    return pl.pallas_call(
        back_kernel,
        out_shape=(shape((HEADS, TOK, DIM), BF), half, half),
        in_specs=[scalars()] + [whole()] * 5 + [anywhere()] * len(earlier),
        out_specs=(whole(),) * 3,
        scratch_shapes=[pltpu.VMEM((2, ROWS, DIM), F32)],
        compiler_params=params(8),
        cost_estimate=cost(2 * TOK * FEAT * COLS + 2 * HEADS * TOK * DIM * DIM, 15 * MIB),
        name="back",
    )(place, cotangent, weight, attn, qh, docs, *earlier)


def block_rows(place, keep_ref, got_ref, a):
    y, z, c, x = place[0], place[1], place[2], place[3]
    rows = []
    for b in range(4):
        to_y = lax.rem(y + jnp.where(c == 0, a, b), 4)
        to_z = lax.rem(z + jnp.where(c == 0, b, a), 4)
        r = lax.rem(to_y + 4 - x, 4)
        rows.append(jnp.concatenate([keep_ref[r, to_z], got_ref[r, to_z]], 1))
    return jnp.concatenate(rows, 0)


def far_terms_kernel(place, keep_ref, got_ref, normed_ref, normed2_ref, *rest):
    up_ref, down_ref = rest[-2:]
    rows = block_rows(place, keep_ref, got_ref, 2)
    total = dot(rows[:, :TOK], normed_ref[...], 1, 0) + dot(rows[:, TOK:], normed2_ref[...], 1, 0)
    up_ref[...] = total[:192].astype(BF)
    down_ref[...] = total[192:].astype(BF)


def far_terms(place, keep, got, normed, normed2, *earlier):
    out = shape((192, FEAT), BF)
    return pl.pallas_call(
        far_terms_kernel,
        out_shape=(out, out),
        in_specs=[scalars()] + [whole()] * 4 + [anywhere()] * len(earlier),
        out_specs=(whole(), whole()),
        compiler_params=params(10),
        cost_estimate=cost(TOK * FEAT * COLS // 2, 6 * MIB),
        name="far_terms",
    )(place, keep, got, normed, normed2, *earlier)


def near_terms_kernel(place, keep_ref, got_ref, normed_ref, normed2_ref, *rest):
    out_ref = rest[-1]
    for slot, a in ((0, 1), (1, 3), (2, 0)):
        rows = block_rows(place, keep_ref, got_ref, a)
        part = dot(rows[:, :TOK], normed_ref[...], 1, 0)
        out_ref[slot] = part + dot(rows[:, TOK:], normed2_ref[...], 1, 0)


def near_terms(place, keep, got, normed, normed2, *earlier):
    return pl.pallas_call(
        near_terms_kernel,
        out_shape=shape((3, 384, FEAT), F32),
        in_specs=[scalars()] + [whole()] * 4 + [anywhere()] * len(earlier),
        out_specs=whole(),
        compiler_params=params(12),
        cost_estimate=cost(3 * TOK * FEAT * COLS // 2, 10 * MIB),
        name="near_terms",
    )(place, keep, got, normed, normed2, *earlier)


def inner_kernel(group, place, scores_ref, q_ref, k_ref, v_ref, grad_ref, keep_ref, take_ref, doc_ref, docs_ref, *rest):
    gq_ref, gk_ref, gv_ref, mask, turned = rest[-5:]
    n = pl.program_id(0)

    @pl.when(n == 0)
    def _():
        before, after = causal(docs_ref)
        mask[...] = before.astype(BF)
        turned[...] = after.astype(BF)

    c = place[2]
    reads = (upright(docs_ref[...], DIM) == doc_ref[:1]).astype(F32)
    mid = TOK // 2
    for j in range(2):
        q, k, v, grad = q_ref[j], k_ref[j], v_ref[j], grad_ref[j]
        spot = pl.multiple_of((n * 2 + j) * DIM, DIM)
        state = jnp.where(c == group, keep_ref[pl.ds(spot, DIM)], take_ref[pl.ds(spot, DIM)])
        across = reads * dot(grad, state, 1, 1)
        for rows, width in ((slice(0, mid), mid), (slice(mid, TOK), TOK)):
            scores = dot(grad[rows], v[:width], 1, 1).astype(BF) * mask[rows, :width]
            gq_ref[j, rows] = (dot(scores, k[:width], 1, 0) + across[rows]).astype(BF)
        for rows, start in ((slice(0, mid), 0), (slice(mid, TOK), mid)):
            scores = dot(v[rows], grad[start:], 1, 1).astype(BF) * turned[rows, start:]
            gk_ref[j, rows] = dot(scores, q[start:], 1, 0)
            gv_ref[j, rows] = dot(scores_ref[j, rows, start:], grad[start:], 1, 0)


def inner(group, place, scores, qh, kh, vh, grad, keep, take, doc, docs, *earlier):
    def kernel(*refs):
        inner_kernel(group, *refs)

    head = pl.BlockSpec((2, TOK, DIM), lambda n: (n + group * HALF // 2, 0, 0))
    out = pl.BlockSpec((2, TOK, DIM), lambda n: (n, 0, 0))
    return pl.pallas_call(
        kernel,
        grid=(HALF // 2,),
        out_shape=(shape((HALF, TOK, DIM), BF),) + (shape((HALF, TOK, DIM), F32),) * 2,
        in_specs=[scalars(), pl.BlockSpec((2, TOK, TOK), lambda n: (n + group * HALF // 2, 0, 0))]
        + [head] * 4
        + [fixed(ROWS, DIM)] * 2
        + [fixed(8, DIM), fixed(1, TOK)]
        + [anywhere()] * len(earlier),
        out_specs=(out, out, out),
        scratch_shapes=[pltpu.VMEM((TOK, TOK), BF), pltpu.VMEM((TOK, TOK), BF)],
        compiler_params=params(14),
        cost_estimate=cost(5 * HEADS * TOK * TOK * DIM, 5 * MIB),
        name="inner",
    )(place, scores, qh, kh, vh, grad, keep, take, doc, docs, *earlier)


def last_kernel(place, k_ref, v_ref, gq0, gk0, gv0, gq1, gk1, gv1, keep_ref, take_ref, doc_ref, docs_ref, *rest):
    out_q, out_k, out_v, held_k, held_v = rest[-5:]
    c = place[2]
    writes = (upright(docs_ref[...], DIM) == doc_ref[:1]).astype(F32)
    for h in range(HEADS):
        state = pick_state(c, keep_ref, take_ref, h)
        gk, gv = ((gk0, gv0), (gk1, gv1))[h // HALF]
        held_k[h] = (gk[h % HALF] + writes * dot(v_ref[h], state, 1, 1)).astype(BF)
        held_v[h] = (gv[h % HALF] + writes * dot(k_ref[h], state, 1, 0)).astype(BF)
    out_q[...] = jnp.swapaxes(jnp.concatenate([gq0[...], gq1[...]], 0), 0, 1)
    out_k[...] = jnp.swapaxes(held_k[...], 0, 1)
    out_v[...] = jnp.swapaxes(held_v[...], 0, 1)


def last(place, kh, vh, lower, upper, keep, take, doc, docs, *earlier):
    out = shape((TOK, HEADS, DIM), BF)
    return pl.pallas_call(
        last_kernel,
        out_shape=(out, out, out),
        in_specs=[scalars()] + [whole()] * 12 + [anywhere()] * len(earlier),
        out_specs=(whole(),) * 3,
        scratch_shapes=[pltpu.VMEM((HEADS, TOK, DIM), BF)] * 2,
        compiler_params=params(12),
        cost_estimate=cost(4 * HEADS * TOK * DIM * DIM, 9 * MIB),
        name="last",
    )(place, kh, vh, *lower, *upper, keep, take, doc, docs, *earlier)


def pass_kernel(terms_ref, up_ref, down_ref, out_right, out_left):
    rows = up_ref.shape[0]
    out_right[:rows] = (terms_ref[0, :rows] + up_ref[...].astype(F32)).astype(BF)
    out_right[rows:] = terms_ref[0, rows:].astype(BF)
    out_left[:rows] = terms_ref[1, :rows].astype(BF)
    out_left[rows:] = (terms_ref[1, rows:] + down_ref[...].astype(F32)).astype(BF)


def pass_on(terms, up, down):
    out = shape((384, FEAT), BF)
    return pl.pallas_call(
        pass_kernel,
        grid=(1,),
        out_shape=(out, out),
        in_specs=[pl.BlockSpec((2, 384, FEAT), lambda n: (0, 0, 0)), fixed(192, FEAT), fixed(192, FEAT)],
        out_specs=(fixed(384, FEAT), fixed(384, FEAT)),
        compiler_params=params(16),
        cost_estimate=cost(384 * FEAT * 2, 5 * MIB),
        name="pass_on",
    )(terms, up, down)


def middle_kernel(own_ref, left_ref, right_ref, own_out, *outs):
    total = own_ref[...] + left_ref[...].astype(F32) + right_ref[...].astype(F32)
    own_out[...] = total[:96]
    for b in (1, 2, 3):
        outs[b - 1][...] = total[96 * b : 96 * (b + 1)].astype(BF)


def middle(terms, from_left, from_right):
    small = shape((96, FEAT), BF)
    return pl.pallas_call(
        middle_kernel,
        grid=(1,),
        out_shape=(shape((96, FEAT), F32), small, small, small),
        in_specs=[
            pl.BlockSpec((pl.squeezed, 384, FEAT), lambda n: (2, 0, 0)),
            fixed(384, FEAT),
            fixed(384, FEAT),
        ],
        out_specs=(fixed(96, FEAT),) * 4,
        compiler_params=params(16),
        cost_estimate=cost(384 * FEAT * 2, 4 * MIB),
        name="middle",
    )(terms, from_left, from_right)


def hold_kernel(share_ref, *rest):
    rest[-1][...] = share_ref[...]


def hold(share, *earlier):
    return pl.pallas_call(
        hold_kernel,
        out_shape=shape(share.shape, BF),
        in_specs=[whole()] + [anywhere()] * len(earlier),
        out_specs=whole(),
        compiler_params=params(4),
        cost_estimate=cost(96 * FEAT, MIB),
        name="hold",
    )(share, *earlier)


def end_kernel(own_ref, p1, p2, p3, out_ref):
    out_ref[...] = own_ref[...] + p1[...].astype(F32) + p2[...].astype(F32) + p3[...].astype(F32)


def end(own, parts):
    return pl.pallas_call(
        end_kernel,
        grid=(1,),
        out_shape=shape((96, FEAT), F32),
        in_specs=[fixed(96, FEAT)] * 4,
        out_specs=fixed(96, FEAT),
        compiler_params=params(8),
        cost_estimate=cost(96 * FEAT * 3, MIB),
        name="end",
    )(own, *parts)


def route(move):
    pairs = []
    for i in range(32):
        target = move(i // 8, (i // 2) % 4, i % 2)
        if target is not None:
            y, z, c = target
            pairs.append((i, ((y % 4) * 4 + z % 4) * 2 + c))
    return pairs


SWAP = route(lambda y, z, c: (y, z, 1 - c))


def across_z(step):
    return route(lambda y, z, c: (y, z ^ step, c))


def across_y(step):
    return route(lambda y, z, c: (y ^ step, z, c))


def along_y_open(step):
    return route(lambda y, z, c: (y + step, z, c) if 0 <= y + step < 4 else None)


def along_first(step):
    return route(lambda y, z, c: (y + step, z, c) if c == 0 else (y, z + step, c))


def along_second(step):
    return route(lambda y, z, c: (y, z + step, c) if c == 0 else (y + step, z, c))


def send(array, pairs):
    return lax.ppermute(array, "seq", pairs)


def along_head(array, step):
    return lax.ppermute(array, "head", [(i, (i + step) % 4) for i in range(4)])


def shards(queries, key_vectors, value_vectors, doc_ids, out_weight, grad_out):
    i = lax.axis_index("seq")
    place = jnp.stack([i // 8, (i // 2) % 4, i % 2, lax.axis_index("head")]).astype(jnp.int32)
    docs = doc_ids.reshape(1, TOK)
    qh, kh, vh, keep, give, cot = prepare(place, queries, key_vectors, value_vectors, docs, grad_out)
    on_left, on_right = along_head(cot, 1), along_head(cot, -1)
    far, chip = chip_state(place, keep, send(give, SWAP), True)
    beside = send(chip, across_z(1))
    intra0 = intra(qh, kh, vh, docs, 0, far)
    pair = join(place, chip, beside, True, 1, intra0)
    beyond = send(pair, across_z(2))
    scores = upper_scores(qh, kh, docs, pair)
    total = join(place, pair, beyond, True, 2, scores)
    aboves = [send(total, along_y_open(k)) for k in (1, 2)]
    intra1 = intra(qh, kh, vh, docs, 1, total)
    top, bottom = halves(on_left, on_right, intra1)
    mine, theirs, doc = entry_state(place, far, [beside, beyond] + aboves, (1, 2, -1, -2), True, top)
    far_top, far_bottom = along_head(top, 1), along_head(bottom, -1)
    taken = send(theirs, SWAP)
    attn, normed = attend(place, qh, intra0, intra1, mine, taken, doc, docs)
    normed2 = send(normed, SWAP)
    cotangent, blocks, others = turn(place, cot, on_right, far_top, far_bottom, on_left, normed)
    blocks2 = send(others, SWAP)
    grad, keep, give = back(place, cotangent, out_weight, attn, qh, docs, others)
    got = send(give, SWAP)
    far_up, far_down = far_terms(place, blocks, blocks2, normed, normed2, keep)
    up, down = send(far_up, along_first(1)), send(far_down, along_first(-1))
    far, chip = chip_state(place, keep, got, False, far_up)
    steps = [send(chip, across_z(1))]
    top, bottom = project(place, (2,), normed, out_weight, far)
    top, bottom = along_head(top, 1), along_head(bottom, -1)
    terms = near_terms(place, blocks, blocks2, normed, normed2, far)
    joined = join(place, chip, steps[0], False, 1, terms)
    steps.append(send(joined, across_z(2)))
    on, back_on = pass_on(terms, up, down)
    on, back_on = send(on, along_first(1)), send(back_on, along_first(-1))
    right, left, out_own = project(place, (1, 3, 0), normed, out_weight, joined)
    joined = join(place, joined, steps[1], False, 2, right)
    steps.append(send(joined, across_y(1)))
    right, left = out_pass(right, left, top, bottom, joined)
    right, left = along_head(right, 1), along_head(left, -1)
    lower = inner(0, place, scores, qh, kh, vh, grad, mine, taken, doc, docs, joined)
    joined = join(place, joined, steps[2], False, 4, lower[0])
    steps.append(send(joined, across_y(2)))
    upper = inner(1, place, scores, qh, kh, vh, grad, mine, taken, doc, docs, joined)
    back_mine, theirs, back_doc = entry_state(place, far, steps, (1, 2, 4, 8), False, upper[0])
    back_taken = send(theirs, SWAP)
    own, *shares = middle(terms, on, back_on)
    shares[1] = hold(shares[1], theirs)
    shares = [send(share, along_second(k)) for k, share in zip((1, 2, 3), shares)]
    grad_queries, grad_keys, grad_values = last(
        place, kh, vh, lower, upper, back_mine, back_taken, back_doc, docs, own
    )
    layer_out = out_end(out_own, right, left, own)
    grad_weight = end(own, shares).T
    return layer_out, grad_queries, grad_keys, grad_values, grad_weight


def solution(mesh):
    placed = (
        P("seq", "head", None),
        P("seq", "head", None),
        P("seq", "head", None),
        P("seq"),
        P("head", None),
        P("seq", "head"),
    )
    return jax.shard_map(
        shards,
        mesh=mesh,
        in_specs=placed,
        out_specs=(
            P("seq", "head"),
            P("seq", "head", None),
            P("seq", "head", None),
            P("seq", "head", None),
            P("head", "seq"),
        ),
        check_vma=False,
    )
```

profile of v0, /device:TPU:0, one launch (start us, length us, event | category | flops | bytes accessed | tf_op | source)
XLA Modules:
  0.0 111.0 jit_solution(17710411234862278081)
XLA Ops:
  0.8 4.2 %prepare.1 = (bf16[8,512,128]{2,1,0:T(8,128)(2,1)S(1)}, bf16[8,512,128]{2,1,0:T(8,128)(2,1)S(1)}, bf16[8,512,128]{2,1,0:T(8,128)(2,1)S(1)}, f32[520,128]{1,0:T(8...) custom-call(s32[4]{0:T(128)S(1)} %pad_add_fusion.place.refs_0_, bf16[512,8,128]{2,1,0:T(8,128)(2,1)} %q_hbm.1, ...), custom_call_target="tpu_custom_call" | custom-call | flops 134217728 | bytes 6291456 | tf_op jit(solution)/shard_map/prepare/pallas_call | solution.py:111
  4.9 1.6 %collective-permute-start.5 = (bf16[512,768]{1,0:T(8,128)(2,1)S(1)}, bf16[512,768]{1,0:T(8,128)(2,1)S(1)}, u32[]{:S(2)}, u32[]{:S(2)}) collective-permute-start(bf16[512,768]{1,0:T(8,128)(2,1)S(1)} %get-tuple-element.62.own_ref), channel_id=1, source_target_pairs={{0,1},{1,2},{2,3},{3,0},{4,5},{5,6},{6,7},{7,4},{8,9},{9,10},{10,1... | collective-permute-start | bytes 2359304 | tf_op jit(solution)/shard_map/ppermute | solution.py:765
  6.6 1.7 %collective-permute-start.6 = (bf16[512,768]{1,0:T(8,128)(2,1)S(1)}, bf16[512,768]{1,0:T(8,128)(2,1)S(1)}, u32[]{:S(2)}, u32[]{:S(2)}) collective-permute-start(bf16[512,768]{1,0:T(8,128)(2,1)S(1)} %get-tuple-element.62.own_ref), channel_id=1, source_target_pairs={{0,3},{1,0},{2,1},{3,2},{4,7},{5,4},{6,5},{7,6},{8,11},{9,8},{10,9... | collective-permute-start | bytes 2359304 | tf_op jit(solution)/shard_map/ppermute | solution.py:765
  8.2 1.5 %collective-permute-done.refs_2_ = f32[520,128]{1,0:T(8,128)S(1)} collective-permute-done((f32[520,128]{1,0:T(8,128)S(1)}, f32[520,128]{1,0:T(8,128)S(1)}, u32[]{:S(2)}, u32[]{:S(2)}) %collective-permute-start) | collective-permute-done | bytes 266272 | tf_op jit(solution)/shard_map/ppermute | solution.py:761
  10.4 2.1 %collective-permute-start.1 = (bf16[528,128]{1,0:T(8,128)(2,1)S(1)}, bf16[528,128]{1,0:T(8,128)(2,1)S(1)}, u32[]{:S(2)}, u32[]{:S(2)}) collective-permute-start(bf16[528,128]{1,0:T(8,128)(2,1)S(1)} %get-tuple-element.61.refs_1_), channel_id=1, source_target_pairs={{0,8},{4,12},{8,0},{12,4},{16,24},{20,28},{24,16},{28,20},{32,40},... | collective-permute-start | bytes 405512 | tf_op jit(solution)/shard_map/ppermute | solution.py:761
  12.5 1.4 %intra.2.refs_3_.intra0 = f32[4,512,128]{2,1,0:T(8,128)S(1)} custom-call(bf16[8,512,128]{2,1,0:T(8,128)(2,1)S(1)} %get-tuple-element.55.q_ref.refs_2_, bf16[8,512,128]{2,1,0:T(8,128)(2,1)S(1)} %get-tuple-element.56.k_ref.refs_3_, bf16[8,512,128]{2,1,0:T(8,128)(2,1)S(1)} %get-tuple-element.57.v_ref.refs_4_, s32[1,512]{1,0:T(1,128)S(1)} %bitcast.9, ...), custom_call_target="tpu_custom_call" | custom-call | flops 536870912 | bytes 3145728 | tf_op jit(solution)/shard_map/intra/pallas_call | solution.py:274
  13.9 2.4 %collective-permute-done.1.refs_2_ = bf16[528,128]{1,0:T(8,128)(2,1)S(1)} collective-permute-done((bf16[528,128]{1,0:T(8,128)(2,1)S(1)}, bf16[528,128]{1,0:T(8,128)(2,1)S(1)}, u32[]{:S(2)}, u32[]{:S(2)}) %collective-permute-start.1) | collective-permute-done | bytes 135200 | tf_op jit(solution)/shard_map/ppermute | solution.py:761
  17.0 3.8 %collective-permute-start.2 = (bf16[528,128]{1,0:T(8,128)(2,1)S(1)}, bf16[528,128]{1,0:T(8,128)(2,1)S(1)}, u32[]{:S(2)}, u32[]{:S(2)}) collective-permute-start(bf16[528,128]{1,0:T(8,128)(2,1)S(1)} %join.5.rest_0_.refs_1_), channel_id=1, source_target_pairs={{0,16},{4,20},{8,24},{12,28},{16,0},{20,4},{24,8},{28,12},{32,48},... | collective-permute-start | bytes 405512 | tf_op jit(solution)/shard_map/ppermute | solution.py:761
  20.7 1.0 upper_scores.1.refs_3_.refs_1_
  21.7 2.1 %collective-permute-done.2.refs_2_.refs_3_ = bf16[528,128]{1,0:T(8,128)(2,1)S(1)} collective-permute-done((bf16[528,128]{1,0:T(8,128)(2,1)S(1)}, bf16[528,128]{1,0:T(8,128)(2,1)S(1)}, u32[]{:S(2)}, u32[]{:S(2)}) %collective-permute-start.2) | collective-permute-done | bytes 135200 | tf_op jit(solution)/shard_map/ppermute | solution.py:761
  24.4 1.5 %intra.3.rest_0_.intra1 = f32[4,512,128]{2,1,0:T(8,128)S(1)} custom-call(bf16[8,512,128]{2,1,0:T(8,128)(2,1)S(1)} %get-tuple-element.55.q_ref.refs_2_, bf16[8,512,128]{2,1,0:T(8,128)(2,1)S(1)} %get-tuple-element.56.k_ref.refs_3_, bf16[8,512,128]{2,1,0:T(8,128)(2,1)S(1)} %get-tuple-element.57.v_ref.refs_4_, s32[1,512]{1,0:T(1,128)S(1)} %bitcast.11, ...), custom_call_target="tpu_custom_call" | custom-call | flops 536870912 | bytes 3145728 | tf_op jit(solution)/shard_map/intra/pallas_call | solution.py:274
  26.0 1.2 %collective-permute-start.8 = (bf16[256,768]{1,0:T(8,128)(2,1)S(1)}, bf16[256,768]{1,0:T(8,128)(2,1)S(1)}, u32[]{:S(2)}, u32[]{:S(2)}) collective-permute-start(bf16[256,768]{1,0:T(8,128)(2,1)S(1)} %get-tuple-element.63.refs_6_), channel_id=1, source_target_pairs={{0,1},{1,2},{2,3},{3,0},{4,5},{5,6},{6,7},{7,4},{8,9},{9,10},{10,1... | collective-permute-start | bytes 1179656 | tf_op jit(solution)/shard_map/ppermute | solution.py:765
  27.2 2.1 %collective-permute-start.9 = (bf16[256,768]{1,0:T(8,128)(2,1)S(1)}, bf16[256,768]{1,0:T(8,128)(2,1)S(1)}, u32[]{:S(2)}, u32[]{:S(2)}) collective-permute-start(bf16[256,768]{1,0:T(8,128)(2,1)S(1)} %get-tuple-element.68), channel_id=1, source_target_pairs={{0,3},{1,0},{2,1},{3,2},{4,7},{5,4},{6,5},{7,6},{8,11},{9,8},{10,9... | collective-permute-start | bytes 1179656 | tf_op jit(solution)/shard_map/ppermute | solution.py:765
  29.3 3.5 %collective-permute-start.3 = (bf16[528,128]{1,0:T(8,128)(2,1)S(1)}, bf16[528,128]{1,0:T(8,128)(2,1)S(1)}, u32[]{:S(2)}, u32[]{:S(2)}) collective-permute-start(bf16[528,128]{1,0:T(8,128)(2,1)S(1)} %join.6.rest_0_), channel_id=1, source_target_pairs={{0,32},{4,36},{8,40},{12,44},{16,48},{20,52},{24,56},{28,60},{32,6... | collective-permute-start | bytes 405512 | tf_op jit(solution)/shard_map/ppermute | solution.py:761
  32.7 4.8 %collective-permute-start.4 = (bf16[528,128]{1,0:T(8,128)(2,1)S(1)}, bf16[528,128]{1,0:T(8,128)(2,1)S(1)}, u32[]{:S(2)}, u32[]{:S(2)}) collective-permute-start(bf16[528,128]{1,0:T(8,128)(2,1)S(1)} %join.6.rest_0_), channel_id=1, source_target_pairs={{0,64},{4,68},{8,72},{12,76},{16,80},{20,84},{24,88},{28,92},{32,9... | collective-permute-start | bytes 405512 | tf_op jit(solution)/shard_map/ppermute | solution.py:761
  37.6 2.5 %collective-permute-done.4.refs_5_ = bf16[528,128]{1,0:T(8,128)(2,1)S(1)} collective-permute-done((bf16[528,128]{1,0:T(8,128)(2,1)S(1)}, bf16[528,128]{1,0:T(8,128)(2,1)S(1)}, u32[]{:S(2)}, u32[]{:S(2)}) %collective-permute-start.4) | collective-permute-done | bytes 135200 | tf_op jit(solution)/shard_map/ppermute | solution.py:761
  40.1 0.7 entry_state.2
  40.9 1.3 %collective-permute-done.7.take_ref.refs_7_ = bf16[512,128]{1,0:T(8,128)(2,1)S(1)} collective-permute-done((bf16[512,128]{1,0:T(8,128)(2,1)S(1)}, bf16[512,128]{1,0:T(8,128)(2,1)S(1)}, u32[]{:S(2)}, u32[]{:S(2)}) %collective-permute-start.7) | collective-permute-done | bytes 131104 | tf_op jit(solution)/shard_map/ppermute | solution.py:761
  42.3 1.5 %attend.1 = (f32[8,512,128]{2,1,0:T(8,128)S(1)}, bf16[512,1024]{1,0:T(8,128)(2,1)S(1)}) custom-call(s32[4]{0:T(128)S(1)} %pad_add_fusion.place.refs_0_, bf16[8,512,128]{2,1,0:T(8,128)(2,1)S(1)} %get-tuple-element.55.q_ref.refs_2_, f32[4,512,128]{2,1,0:T(8,128)S(1)} %intra.2.refs_3_.intra0, f32[4,512,128]{2,1,0:T(8,128)S(1)} %intra.3.rest_0_.intra1, ...), custom_call_target="tpu_custom_call" | custom-call | flops 134217728 | bytes 6291456 | tf_op jit(solution)/shard_map/attend/pallas_call | solution.py:329
  43.8 1.5 %turn.1 = (bf16[512,3072]{1,0:T(8,128)(2,1)S(1)}, bf16[4,4,96,512]{3,2,1,0:T(8,128)(2,1)S(1)}, bf16[4,4,96,512]{3,2,1,0:T(8,128)(2,1)S(1)}) custom-call(s32[4]{0:T(128)S(1)} %pad_add_fusion.place.refs_0_, bf16[512,768]{1,0:T(8,128)(2,1)S(1)} %get-tuple-element.62.own_ref, bf16[512,768]{1,0:T(8,128)(2,1)S(1)} %collective-permute-done.6.right_ref, ...), custom_call_target="tpu_custom_call" | custom-call | flops 1572864 | bytes 6291456 | tf_op jit(solution)/shard_map/turn/pallas_call | solution.py:465
  45.9 8.5 %back.1 = (bf16[8,512,128]{2,1,0:T(8,128)(2,1)S(1)}, f32[520,128]{1,0:T(8,128)S(1)}, f32[520,128]{1,0:T(8,128)S(1)}) custom-call(s32[4]{0:T(128)S(1)} %pad_add_fusion.place.refs_0_, bf16[512,3072]{1,0:T(8,128)(2,1)S(1)} %get-tuple-element.69.cot_ref, bf16[1024,3072]{1,0:T(8,128)(2,1)S(1)} %bitcast.7, f32[8,512,128]{2,1,0:T(8,128)S(1)} %get-tuple-element.70.attn_ref, ...), custom_call_target="tpu_custom_call" | custom-call | flops 3355443200 | bytes 15728640 | tf_op jit(solution)/shard_map/back/pallas_call | solution.py:505
  54.8 1.5 %far_terms.1 = (bf16[192,1024]{1,0:T(8,128)(2,1)S(1)}, bf16[192,1024]{1,0:T(8,128)(2,1)S(1)}) custom-call(s32[4]{0:T(128)S(1)} %pad_add_fusion.place.refs_0_, bf16[4,4,96,512]{3,2,1,0:T(8,128)(2,1)S(1)} %get-tuple-element.74.keep_ref, bf16[4,4,96,512]{3,2,1,0:T(8,128)(2,1)S(1)} %collective-permute-done.11.got_ref, ...), custom_call_target="tpu_custom_call" | custom-call | flops 805306368 | bytes 6291456 | tf_op jit(solution)/shard_map/far_terms/pallas_call | solution.py:538
  56.4 3.2 %collective-permute-start.20 = (bf16[192,1024]{1,0:T(8,128)(2,1)S(1)}, bf16[192,1024]{1,0:T(8,128)(2,1)S(1)}, u32[]{:S(2)}, u32[]{:S(2)}) collective-permute-start(bf16[192,1024]{1,0:T(8,128)(2,1)S(1)} %get-tuple-element.85), channel_id=1, source_target_pairs={{0,96},{4,28},{8,104},{12,4},{16,112},{20,12},{24,120},{28,20},{32... | collective-permute-start | bytes 1179656 | tf_op jit(solution)/shard_map/ppermute | solution.py:761
  59.6 0.6 chip_state.3
  60.2 1.7 %collective-permute-start.13 = (bf16[528,128]{1,0:T(8,128)(2,1)S(1)}, bf16[528,128]{1,0:T(8,128)(2,1)S(1)}, u32[]{:S(2)}, u32[]{:S(2)}) collective-permute-start(bf16[528,128]{1,0:T(8,128)(2,1)S(1)} %get-tuple-element.76.refs_1_), channel_id=1, source_target_pairs={{0,8},{4,12},{8,0},{12,4},{16,24},{20,28},{24,16},{28,20},{32,40},... | collective-permute-start | bytes 405512 | tf_op jit(solution)/shard_map/ppermute | solution.py:761
  61.9 1.8 %project.3 = (bf16[256,768]{1,0:T(8,128)(2,1)S(1)}, bf16[256,768]{1,0:T(8,128)(2,1)S(1)}) custom-call(s32[4]{0:T(128)S(1)} %pad_add_fusion.place.refs_0_, bf16[512,1024]{1,0:T(8,128)(2,1)S(1)} %get-tuple-element.67.rest_0_.normed_ref.refs_1_, bf16[1024,3072]{1,0:T(8,128)(2,1)S(1)} %bitcast.7, f32[520,128]{1,0:T(8,128)S(1)} %get-tuple-element.77.rest_0_.refs_3_.refs_1_), custom_call_target="tpu_custom_call" | custom-call | flops 805306368 | bytes 3145728 | tf_op jit(solution)/shard_map/project/pallas_call | solution.py:372
  64.0 2.9 %collective-permute-start.15 = (bf16[256,768]{1,0:T(8,128)(2,1)S(1)}, bf16[256,768]{1,0:T(8,128)(2,1)S(1)}, u32[]{:S(2)}, u32[]{:S(2)}) collective-permute-start(bf16[256,768]{1,0:T(8,128)(2,1)S(1)} %get-tuple-element.82), channel_id=1, source_target_pairs={{0,3},{1,0},{2,1},{3,2},{4,7},{5,4},{6,5},{7,6},{8,11},{9,8},{10,9... | collective-permute-start | bytes 1179656 | tf_op jit(solution)/shard_map/ppermute | solution.py:765
  67.0 3.2 %near_terms.1.refs_3_.terms_ref.own_ref = f32[3,384,1024]{2,1,0:T(8,128)S(1)} custom-call(s32[4]{0:T(128)S(1)} %pad_add_fusion.place.refs_0_, bf16[4,4,96,512]{3,2,1,0:T(8,128)(2,1)S(1)} %get-tuple-element.74.keep_ref, bf16[4,4,96,512]{3,2,1,0:T(8,128)(2,1)S(1)} %collective-permute-done.11.got_ref, ...), custom_call_target="tpu_custom_call" | custom-call | flops 2415919104 | bytes 10485760 | tf_op jit(solution)/shard_map/near_terms/pallas_call | solution.py:558
  70.8 3.7 %collective-permute-start.16 = (bf16[528,128]{1,0:T(8,128)(2,1)S(1)}, bf16[528,128]{1,0:T(8,128)(2,1)S(1)}, u32[]{:S(2)}, u32[]{:S(2)}) collective-permute-start(bf16[528,128]{1,0:T(8,128)(2,1)S(1)} %join.7.refs_3_.refs_1_), channel_id=1, source_target_pairs={{0,16},{4,20},{8,24},{12,28},{16,0},{20,4},{24,8},{28,12},{32,48},... | collective-permute-start | bytes 405512 | tf_op jit(solution)/shard_map/ppermute | solution.py:761
  74.6 0.8 collective-permute-start.21
  75.4 2.6 %collective-permute-start.22 = (bf16[384,1024]{1,0:T(8,128)(2,1)S(1)}, bf16[384,1024]{1,0:T(8,128)(2,1)S(1)}, u32[]{:S(2)}, u32[]{:S(2)}) collective-permute-start(bf16[384,1024]{1,0:T(8,128)(2,1)S(1)} %get-tuple-element.87), channel_id=1, source_target_pairs={{0,96},{4,28},{8,104},{12,4},{16,112},{20,12},{24,120},{28,20},{32... | collective-permute-start | bytes 2359304 | tf_op jit(solution)/shard_map/ppermute | solution.py:761
  78.0 4.7 %project.2 = (bf16[512,768]{1,0:T(8,128)(2,1)S(1)}, bf16[512,768]{1,0:T(8,128)(2,1)S(1)}, f32[512,768]{1,0:T(8,128)S(1)}) custom-call(s32[4]{0:T(128)S(1)} %pad_add_fusion.place.refs_0_, bf16[512,1024]{1,0:T(8,128)(2,1)S(1)} %get-tuple-element.67.rest_0_.normed_ref.refs_1_, bf16[1024,3072]{1,0:T(8,128)(2,1)S(1)} %bitcast.7, ...), custom_call_target="tpu_custom_call" | custom-call | flops 2415919104 | bytes 9437184 | tf_op jit(solution)/shard_map/project/pallas_call | solution.py:372
  82.7 0.6 join.8.rest_0_.refs_10_.refs_1_
  83.6 3.2 %collective-permute-start.18 = (bf16[512,768]{1,0:T(8,128)(2,1)S(1)}, bf16[512,768]{1,0:T(8,128)(2,1)S(1)}, u32[]{:S(2)}, u32[]{:S(2)}) collective-permute-start(bf16[512,768]{1,0:T(8,128)(2,1)S(1)} %get-tuple-element.84), channel_id=1, source_target_pairs={{0,3},{1,0},{2,1},{3,2},{4,7},{5,4},{6,5},{7,6},{8,11},{9,8},{10,9... | collective-permute-start | bytes 2359304 | tf_op jit(solution)/shard_map/ppermute | solution.py:765
  86.8 3.8 %inner.2 = (bf16[4,512,128]{2,1,0:T(8,128)(2,1)S(1)}, f32[4,512,128]{2,1,0:T(8,128)S(1)}, f32[4,512,128]{2,1,0:T(8,128)S(1)}) custom-call(s32[4]{0:T(128)S(1)} %pad_add_fusion.place.refs_0_, bf16[8,512,512]{2,1,0:T(8,128)(2,1)S(1)} %upper_scores.1.refs_3_.refs_1_, bf16[8,512,128]{2,1,0:T(8,128)(2,1)S(1)} %get-tuple-element.55.q_ref.refs_2_, ...), custom_call_target="tpu_custom_call" | custom-call | flops 1342177280 | bytes 5242880 | tf_op jit(solution)/shard_map/inner/pallas_call | solution.py:602
  90.7 1.2 %collective-permute-done.23.refs_2_.refs_4_ = bf16[528,128]{1,0:T(8,128)(2,1)S(1)} collective-permute-done((bf16[528,128]{1,0:T(8,128)(2,1)S(1)}, bf16[528,128]{1,0:T(8,128)(2,1)S(1)}, u32[]{:S(2)}, u32[]{:S(2)}) %collective-permute-start.23) | collective-permute-done | bytes 135200 | tf_op jit(solution)/shard_map/ppermute | solution.py:761
  91.8 0.6 join.9.refs_10_
  92.4 1.6 %collective-permute-start.24 = (bf16[528,128]{1,0:T(8,128)(2,1)S(1)}, bf16[528,128]{1,0:T(8,128)(2,1)S(1)}, u32[]{:S(2)}, u32[]{:S(2)}) collective-permute-start(bf16[528,128]{1,0:T(8,128)(2,1)S(1)} %join.9.refs_10_), channel_id=1, source_target_pairs={{0,64},{4,68},{8,72},{12,76},{16,80},{20,84},{24,88},{28,92},{32,9... | collective-permute-start | bytes 405512 | tf_op jit(solution)/shard_map/ppermute | solution.py:761
  94.1 3.9 %inner.3 = (bf16[4,512,128]{2,1,0:T(8,128)(2,1)S(1)}, f32[4,512,128]{2,1,0:T(8,128)S(1)}, f32[4,512,128]{2,1,0:T(8,128)S(1)}) custom-call(s32[4]{0:T(128)S(1)} %pad_add_fusion.place.refs_0_, bf16[8,512,512]{2,1,0:T(8,128)(2,1)S(1)} %upper_scores.1.refs_3_.refs_1_, bf16[8,512,128]{2,1,0:T(8,128)(2,1)S(1)} %get-tuple-element.55.q_ref.refs_2_, ...), custom_call_target="tpu_custom_call" | custom-call | flops 1342177280 | bytes 5242880 | tf_op jit(solution)/shard_map/inner/pallas_call | solution.py:602
  97.9 1.1 %collective-permute-done.24.refs_5_ = bf16[528,128]{1,0:T(8,128)(2,1)S(1)} collective-permute-done((bf16[528,128]{1,0:T(8,128)(2,1)S(1)}, bf16[528,128]{1,0:T(8,128)(2,1)S(1)}, u32[]{:S(2)}, u32[]{:S(2)}) %collective-permute-start.24) | collective-permute-done | bytes 135200 | tf_op jit(solution)/shard_map/ppermute | solution.py:761
  99.0 0.8 entry_state.3
  100.2 1.0 collective-permute-start.27
  101.2 2.3 %collective-permute-start.28 = (bf16[96,1024]{1,0:T(8,128)(2,1)S(1)}, bf16[96,1024]{1,0:T(8,128)(2,1)S(1)}, u32[]{:S(2)}, u32[]{:S(2)}) collective-permute-start(bf16[96,1024]{1,0:T(8,128)(2,1)S(1)} %get-tuple-element.104), channel_id=1, source_target_pairs={{0,24},{4,100},{8,0},{12,108},{16,8},{20,116},{24,16},{28,124},{32... | collective-permute-start | bytes 589832 | tf_op jit(solution)/shard_map/ppermute | solution.py:761
  103.6 1.2 %out_end.1 = bf16[512,768]{1,0:T(8,128)(2,1)} custom-call(f32[512,768]{1,0:T(8,128)S(1)} %get-tuple-element.78.own_ref, bf16[512,768]{1,0:T(8,128)(2,1)S(1)} %collective-permute-done.17.left_ref, bf16[512,768]{1,0:T(8,128)(2,1)S(1)} %collective-permute-done.18.right_ref, f32[96,1024]{1,0:T(8,128)S(1)} %get-tuple-element.88.rest_0_.own_ref), custom_call_target="tpu_custom_call" | custom-call | flops 786432 | bytes 4194304 | tf_op jit(solution)/shard_map/out_end/pallas_call | solution.py:432
  104.9 3.1 %last.1 = (bf16[512,8,128]{2,1,0:T(8,128)(2,1)}, bf16[512,8,128]{2,1,0:T(8,128)(2,1)}, bf16[512,8,128]{2,1,0:T(8,128)(2,1)}) custom-call(s32[4]{0:T(128)S(1)} %pad_add_fusion.place.refs_0_, bf16[8,512,128]{2,1,0:T(8,128)(2,1)S(1)} %get-tuple-element.56.k_ref.refs_3_, bf16[8,512,128]{2,1,0:T(8,128)(2,1)S(1)} %get-tuple-element.57.v_ref.refs_4_, ...), custom_call_target="tpu_custom_call" | custom-call | flops 268435456 | bytes 9437184 | tf_op jit(solution)/shard_map/last/pallas_call | solution.py:635
  108.1 1.1 collective-permute-done.26.p1
  109.1 1.0 collective-permute-done.28.p3
  110.1 0.8 end.1
  (48 shorter events, 5.0 us)
Async XLA Ops:
  0.7 11.7 %copy-start = (s32[512]{0:T(512)S(1)}, s32[512]{0:T(512)}, u32[]{:S(2)}) copy-start(s32[512]{0:T(512)} %param.9) | copy-start | bytes 6148
  4.9 20.9 %collective-permute-start.5 = (bf16[512,768]{1,0:T(8,128)(2,1)S(1)}, bf16[512,768]{1,0:T(8,128)(2,1)S(1)}, u32[]{:S(2)}, u32[]{:S(2)}) collective-permute-start(bf16[512,768]{1,0:T(8,128)(2,1)S(1)} %get-tuple-element.62.own_ref), channel_id=1, source_target_pairs={{0,1},{1,2},{2,3},{3,0},{4,5},{5,6},{6,7},{7,4},{8,9},{9,10},{10,1... | collective-permute-start | bytes 2359304 | tf_op jit(solution)/shard_map/ppermute | solution.py:765
  6.6 19.3 %collective-permute-start.6 = (bf16[512,768]{1,0:T(8,128)(2,1)S(1)}, bf16[512,768]{1,0:T(8,128)(2,1)S(1)}, u32[]{:S(2)}, u32[]{:S(2)}) collective-permute-start(bf16[512,768]{1,0:T(8,128)(2,1)S(1)} %get-tuple-element.62.own_ref), channel_id=1, source_target_pairs={{0,3},{1,0},{2,1},{3,2},{4,7},{5,4},{6,5},{7,6},{8,11},{9,8},{10,9... | collective-permute-start | bytes 2359304 | tf_op jit(solution)/shard_map/ppermute | solution.py:765
  8.2 1.5 %collective-permute-start = (f32[520,128]{1,0:T(8,128)S(1)}, f32[520,128]{1,0:T(8,128)S(1)}, u32[]{:S(2)}, u32[]{:S(2)}) collective-permute-start(f32[520,128]{1,0:T(8,128)S(1)} %get-tuple-element.59), channel_id=1, source_target_pairs={{0,4},{4,0},{8,12},{12,8},{16,20},{20,16},{24,28},{28,24},{32,36},... | collective-permute-start | bytes 798728 | tf_op jit(solution)/shard_map/ppermute | solution.py:761
  10.4 6.0 %collective-permute-start.1 = (bf16[528,128]{1,0:T(8,128)(2,1)S(1)}, bf16[528,128]{1,0:T(8,128)(2,1)S(1)}, u32[]{:S(2)}, u32[]{:S(2)}) collective-permute-start(bf16[528,128]{1,0:T(8,128)(2,1)S(1)} %get-tuple-element.61.refs_1_), channel_id=1, source_target_pairs={{0,8},{4,12},{8,0},{12,4},{16,24},{20,28},{24,16},{28,20},{32,40},... | collective-permute-start | bytes 405512 | tf_op jit(solution)/shard_map/ppermute | solution.py:761
  17.0 6.8 %collective-permute-start.2 = (bf16[528,128]{1,0:T(8,128)(2,1)S(1)}, bf16[528,128]{1,0:T(8,128)(2,1)S(1)}, u32[]{:S(2)}, u32[]{:S(2)}) collective-permute-start(bf16[528,128]{1,0:T(8,128)(2,1)S(1)} %join.5.rest_0_.refs_1_), channel_id=1, source_target_pairs={{0,16},{4,20},{8,24},{12,28},{16,0},{20,4},{24,8},{28,12},{32,48},... | collective-permute-start | bytes 405512 | tf_op jit(solution)/shard_map/ppermute | solution.py:761
  25.9 20.0 %slice-start = ((s8[6291456]{0:T(1024)(128)(4,1)}), s8[4194304]{0:T(1024)(128)(4,1)S(1)}, s32[]{:S(2)}) async-start(s8[6291456]{0:T(1024)(128)(4,1)} %bitcast.6), calls=%async_computation | async-start | bytes 8388608
  26.0 17.8 %collective-permute-start.8 = (bf16[256,768]{1,0:T(8,128)(2,1)S(1)}, bf16[256,768]{1,0:T(8,128)(2,1)S(1)}, u32[]{:S(2)}, u32[]{:S(2)}) collective-permute-start(bf16[256,768]{1,0:T(8,128)(2,1)S(1)} %get-tuple-element.63.refs_6_), channel_id=1, source_target_pairs={{0,1},{1,2},{2,3},{3,0},{4,5},{5,6},{6,7},{7,4},{8,9},{9,10},{10,1... | collective-permute-start | bytes 1179656 | tf_op jit(solution)/shard_map/ppermute | solution.py:765
  27.2 16.6 %collective-permute-start.9 = (bf16[256,768]{1,0:T(8,128)(2,1)S(1)}, bf16[256,768]{1,0:T(8,128)(2,1)S(1)}, u32[]{:S(2)}, u32[]{:S(2)}) collective-permute-start(bf16[256,768]{1,0:T(8,128)(2,1)S(1)} %get-tuple-element.68), channel_id=1, source_target_pairs={{0,3},{1,0},{2,1},{3,2},{4,7},{5,4},{6,5},{7,6},{8,11},{9,8},{10,9... | collective-permute-start | bytes 1179656 | tf_op jit(solution)/shard_map/ppermute | solution.py:765
  29.3 8.3 %collective-permute-start.3 = (bf16[528,128]{1,0:T(8,128)(2,1)S(1)}, bf16[528,128]{1,0:T(8,128)(2,1)S(1)}, u32[]{:S(2)}, u32[]{:S(2)}) collective-permute-start(bf16[528,128]{1,0:T(8,128)(2,1)S(1)} %join.6.rest_0_), channel_id=1, source_target_pairs={{0,32},{4,36},{8,40},{12,44},{16,48},{20,52},{24,56},{28,60},{32,6... | collective-permute-start | bytes 405512 | tf_op jit(solution)/shard_map/ppermute | solution.py:761
  32.7 7.3 %collective-permute-start.4 = (bf16[528,128]{1,0:T(8,128)(2,1)S(1)}, bf16[528,128]{1,0:T(8,128)(2,1)S(1)}, u32[]{:S(2)}, u32[]{:S(2)}) collective-permute-start(bf16[528,128]{1,0:T(8,128)(2,1)S(1)} %join.6.rest_0_), channel_id=1, source_target_pairs={{0,64},{4,68},{8,72},{12,76},{16,80},{20,84},{24,88},{28,92},{32,9... | collective-permute-start | bytes 405512 | tf_op jit(solution)/shard_map/ppermute | solution.py:761
  40.8 1.4 %collective-permute-start.7 = (bf16[512,128]{1,0:T(8,128)(2,1)S(1)}, bf16[512,128]{1,0:T(8,128)(2,1)S(1)}, u32[]{:S(2)}, u32[]{:S(2)}) collective-permute-start(bf16[512,128]{1,0:T(8,128)(2,1)S(1)} %get-tuple-element.65), channel_id=1, source_target_pairs={{0,4},{4,0},{8,12},{12,8},{16,20},{20,16},{24,28},{28,24},{32,36},... | collective-permute-start | bytes 393224 | tf_op jit(solution)/shard_map/ppermute | solution.py:761
  42.3 3.6 %slice-start.1 = ((s8[6291456]{0:T(1024)(128)(4,1)}), s8[2097152]{0:T(1024)(128)(4,1)S(1)}, s32[]{:S(2)}) async-start(s8[6291456]{0:T(1024)(128)(4,1)} %bitcast.6), calls=%async_computation.1 | async-start | bytes 4194304
  45.3 9.5 %collective-permute-start.11 = (bf16[4,4,96,512]{3,2,1,0:T(8,128)(2,1)S(1)}, bf16[4,4,96,512]{3,2,1,0:T(8,128)(2,1)S(1)}, u32[]{:S(2)}, u32[]{:S(2)}) collective-permute-start(bf16[4,4,96,512]{3,2,1,0:T(8,128)(2,1)S(1)} %get-tuple-element.71.rest_0_), channel_id=1, source_target_pairs={{0,4},{4,0},{8,12},{12,8},{16,20},{20,16},{24,28},{28,24},{32,36},... | collective-permute-start | bytes 4718600 | tf_op jit(solution)/shard_map/ppermute | solution.py:761
  45.5 9.3 %collective-permute-start.12 = (bf16[512,1024]{1,0:T(8,128)(2,1)S(1)}, bf16[512,1024]{1,0:T(8,128)(2,1)S(1)}, u32[]{:S(2)}, u32[]{:S(2)}) collective-permute-start(bf16[512,1024]{1,0:T(8,128)(2,1)S(1)} %get-tuple-element.67.rest_0_.normed_ref.refs_1_), channel_id=1, source_target_pairs={{0,4},{4,0},{8,12},{12,8},{16,20},{20,16},{24,28},{28,24},{32,36},... | collective-permute-start | bytes 3145736 | tf_op jit(solution)/shard_map/ppermute | solution.py:761
  54.4 5.2 %collective-permute-start.10 = (f32[520,128]{1,0:T(8,128)S(1)}, f32[520,128]{1,0:T(8,128)S(1)}, u32[]{:S(2)}, u32[]{:S(2)}) collective-permute-start(f32[520,128]{1,0:T(8,128)S(1)} %get-tuple-element.73), channel_id=1, source_target_pairs={{0,4},{4,0},{8,12},{12,8},{16,20},{20,16},{24,28},{28,24},{32,36},... | collective-permute-start | bytes 798728 | tf_op jit(solution)/shard_map/ppermute | solution.py:761
  56.3 18.1 %collective-permute-start.19 = (bf16[192,1024]{1,0:T(8,128)(2,1)S(1)}, bf16[192,1024]{1,0:T(8,128)(2,1)S(1)}, u32[]{:S(2)}, u32[]{:S(2)}) collective-permute-start(bf16[192,1024]{1,0:T(8,128)(2,1)S(1)} %get-tuple-element.75.refs_3_), channel_id=1, source_target_pairs={{0,32},{4,12},{8,40},{12,20},{16,48},{20,28},{24,56},{28,4},{32,64... | collective-permute-start | bytes 1179656 | tf_op jit(solution)/shard_map/ppermute | solution.py:761
  56.4 18.0 %collective-permute-start.20 = (bf16[192,1024]{1,0:T(8,128)(2,1)S(1)}, bf16[192,1024]{1,0:T(8,128)(2,1)S(1)}, u32[]{:S(2)}, u32[]{:S(2)}) collective-permute-start(bf16[192,1024]{1,0:T(8,128)(2,1)S(1)} %get-tuple-element.85), channel_id=1, source_target_pairs={{0,96},{4,28},{8,104},{12,4},{16,112},{20,12},{24,120},{28,20},{32... | collective-permute-start | bytes 1179656 | tf_op jit(solution)/shard_map/ppermute | solution.py:761
  60.2 9.9 %collective-permute-start.13 = (bf16[528,128]{1,0:T(8,128)(2,1)S(1)}, bf16[528,128]{1,0:T(8,128)(2,1)S(1)}, u32[]{:S(2)}, u32[]{:S(2)}) collective-permute-start(bf16[528,128]{1,0:T(8,128)(2,1)S(1)} %get-tuple-element.76.refs_1_), channel_id=1, source_target_pairs={{0,8},{4,12},{8,0},{12,4},{16,24},{20,28},{24,16},{28,20},{32,40},... | collective-permute-start | bytes 405512 | tf_op jit(solution)/shard_map/ppermute | solution.py:761
  63.7 19.6 %collective-permute-start.14 = (bf16[256,768]{1,0:T(8,128)(2,1)S(1)}, bf16[256,768]{1,0:T(8,128)(2,1)S(1)}, u32[]{:S(2)}, u32[]{:S(2)}) collective-permute-start(bf16[256,768]{1,0:T(8,128)(2,1)S(1)} %get-tuple-element.81), channel_id=1, source_target_pairs={{0,1},{1,2},{2,3},{3,0},{4,5},{5,6},{6,7},{7,4},{8,9},{9,10},{10,1... | collective-permute-start | bytes 1179656 | tf_op jit(solution)/shard_map/ppermute | solution.py:765
  64.0 19.2 %collective-permute-start.15 = (bf16[256,768]{1,0:T(8,128)(2,1)S(1)}, bf16[256,768]{1,0:T(8,128)(2,1)S(1)}, u32[]{:S(2)}, u32[]{:S(2)}) collective-permute-start(bf16[256,768]{1,0:T(8,128)(2,1)S(1)} %get-tuple-element.82), channel_id=1, source_target_pairs={{0,3},{1,0},{2,1},{3,2},{4,7},{5,4},{6,5},{7,6},{8,11},{9,8},{10,9... | collective-permute-start | bytes 1179656 | tf_op jit(solution)/shard_map/ppermute | solution.py:765
  70.8 11.9 %collective-permute-start.16 = (bf16[528,128]{1,0:T(8,128)(2,1)S(1)}, bf16[528,128]{1,0:T(8,128)(2,1)S(1)}, u32[]{:S(2)}, u32[]{:S(2)}) collective-permute-start(bf16[528,128]{1,0:T(8,128)(2,1)S(1)} %join.7.refs_3_.refs_1_), channel_id=1, source_target_pairs={{0,16},{4,20},{8,24},{12,28},{16,0},{20,4},{24,8},{28,12},{32,48},... | collective-permute-start | bytes 405512 | tf_op jit(solution)/shard_map/ppermute | solution.py:761
  74.6 25.2 %collective-permute-start.21 = (bf16[384,1024]{1,0:T(8,128)(2,1)S(1)}, bf16[384,1024]{1,0:T(8,128)(2,1)S(1)}, u32[]{:S(2)}, u32[]{:S(2)}) collective-permute-start(bf16[384,1024]{1,0:T(8,128)(2,1)S(1)} %get-tuple-element.86), channel_id=1, source_target_pairs={{0,32},{4,12},{8,40},{12,20},{16,48},{20,28},{24,56},{28,4},{32,64... | collective-permute-start | bytes 2359304 | tf_op jit(solution)/shard_map/ppermute | solution.py:761
  75.4 24.4 %collective-permute-start.22 = (bf16[384,1024]{1,0:T(8,128)(2,1)S(1)}, bf16[384,1024]{1,0:T(8,128)(2,1)S(1)}, u32[]{:S(2)}, u32[]{:S(2)}) collective-permute-start(bf16[384,1024]{1,0:T(8,128)(2,1)S(1)} %get-tuple-element.87), channel_id=1, source_target_pairs={{0,96},{4,28},{8,104},{12,4},{16,112},{20,12},{24,120},{28,20},{32... | collective-permute-start | bytes 2359304 | tf_op jit(solution)/shard_map/ppermute | solution.py:761
  83.5 20.0 %collective-permute-start.17 = (bf16[512,768]{1,0:T(8,128)(2,1)S(1)}, bf16[512,768]{1,0:T(8,128)(2,1)S(1)}, u32[]{:S(2)}, u32[]{:S(2)}) collective-permute-start(bf16[512,768]{1,0:T(8,128)(2,1)S(1)} %get-tuple-element.83), channel_id=1, source_target_pairs={{0,1},{1,2},{2,3},{3,0},{4,5},{5,6},{6,7},{7,4},{8,9},{9,10},{10,1... | collective-permute-start | bytes 2359304 | tf_op jit(solution)/shard_map/ppermute | solution.py:765
  83.6 20.0 %collective-permute-start.18 = (bf16[512,768]{1,0:T(8,128)(2,1)S(1)}, bf16[512,768]{1,0:T(8,128)(2,1)S(1)}, u32[]{:S(2)}, u32[]{:S(2)}) collective-permute-start(bf16[512,768]{1,0:T(8,128)(2,1)S(1)} %get-tuple-element.84), channel_id=1, source_target_pairs={{0,3},{1,0},{2,1},{3,2},{4,7},{5,4},{6,5},{7,6},{8,11},{9,8},{10,9... | collective-permute-start | bytes 2359304 | tf_op jit(solution)/shard_map/ppermute | solution.py:765
  86.8 5.0 %collective-permute-start.23 = (bf16[528,128]{1,0:T(8,128)(2,1)S(1)}, bf16[528,128]{1,0:T(8,128)(2,1)S(1)}, u32[]{:S(2)}, u32[]{:S(2)}) collective-permute-start(bf16[528,128]{1,0:T(8,128)(2,1)S(1)} %join.8.rest_0_.refs_10_.refs_1_), channel_id=1, source_target_pairs={{0,32},{4,36},{8,40},{12,44},{16,48},{20,52},{24,56},{28,60},{32,0... | collective-permute-start | bytes 405512 | tf_op jit(solution)/shard_map/ppermute | solution.py:761
  92.4 6.6 %collective-permute-start.24 = (bf16[528,128]{1,0:T(8,128)(2,1)S(1)}, bf16[528,128]{1,0:T(8,128)(2,1)S(1)}, u32[]{:S(2)}, u32[]{:S(2)}) collective-permute-start(bf16[528,128]{1,0:T(8,128)(2,1)S(1)} %join.9.refs_10_), channel_id=1, source_target_pairs={{0,64},{4,68},{8,72},{12,76},{16,80},{20,84},{24,88},{28,92},{32,9... | collective-permute-start | bytes 405512 | tf_op jit(solution)/shard_map/ppermute | solution.py:761
  100.1 9.1 %collective-permute-start.26 = (bf16[96,1024]{1,0:T(8,128)(2,1)S(1)}, bf16[96,1024]{1,0:T(8,128)(2,1)S(1)}, u32[]{:S(2)}, u32[]{:S(2)}) collective-permute-start(bf16[96,1024]{1,0:T(8,128)(2,1)S(1)} %get-tuple-element.102), channel_id=1, source_target_pairs={{0,8},{4,36},{8,16},{12,44},{16,24},{20,52},{24,0},{28,60},{32,40}... | collective-permute-start | bytes 589832 | tf_op jit(solution)/shard_map/ppermute | solution.py:761
  100.2 9.0 %collective-permute-start.27 = (bf16[96,1024]{1,0:T(8,128)(2,1)S(1)}, bf16[96,1024]{1,0:T(8,128)(2,1)S(1)}, u32[]{:S(2)}, u32[]{:S(2)}) collective-permute-start(bf16[96,1024]{1,0:T(8,128)(2,1)S(1)} %hold.1), channel_id=1, source_target_pairs={{0,16},{4,68},{8,24},{12,76},{16,0},{20,84},{24,8},{28,92},{32,48}... | collective-permute-start | bytes 589832 | tf_op jit(solution)/shard_map/ppermute | solution.py:761
  101.2 8.9 %collective-permute-start.28 = (bf16[96,1024]{1,0:T(8,128)(2,1)S(1)}, bf16[96,1024]{1,0:T(8,128)(2,1)S(1)}, u32[]{:S(2)}, u32[]{:S(2)}) collective-permute-start(bf16[96,1024]{1,0:T(8,128)(2,1)S(1)} %get-tuple-element.104), channel_id=1, source_target_pairs={{0,24},{4,100},{8,0},{12,108},{16,8},{20,116},{24,16},{28,124},{32... | collective-permute-start | bytes 589832 | tf_op jit(solution)/shard_map/ppermute | solution.py:761
  103.6 1.3 %collective-permute-start.25 = (bf16[512,128]{1,0:T(8,128)(2,1)S(1)}, bf16[512,128]{1,0:T(8,128)(2,1)S(1)}, u32[]{:S(2)}, u32[]{:S(2)}) collective-permute-start(bf16[512,128]{1,0:T(8,128)(2,1)S(1)} %get-tuple-element.97.rest_0_), channel_id=1, source_target_pairs={{0,4},{4,0},{8,12},{12,8},{16,20},{20,16},{24,28},{28,24},{32,36},... | collective-permute-start | bytes 393224 | tf_op jit(solution)/shard_map/ppermute | solution.py:761
where the time goes:
time: 111 us
  Pallas kernels  50 us (45%)
  starting transfers between devices  45.4 us (41%)
  waiting for transfers between devices  14.4 us (13%)
    ppermute x21, starting transfers between devices, send(): return lax.ppermute(array, 'seq', pairs)  32.2 us
    ppermute x21, waiting for transfers between devices, send(): return lax.ppermute(array, 'seq', pairs)  14.4 us
    ppermute x8, starting transfers between devices, along_head(): return lax.ppermute(array, 'head', [(i, (i + step) % 4) for i in range(4)])  13.2 us
    pallas_call x1, Pallas kernels, back(): pl.pallas_call(back_kernel, out_shape=(shape((HEADS, TOK, DIM), BF), half...  8.54 us
    pallas_call x2, Pallas kernels, inner(): pl.pallas_call(kernel, grid=(HALF // 2,), out_shape=(shape((HALF, TOK, DI...  7.7 us
    pallas_call x2, Pallas kernels, project(): pl.pallas_call(kernel, out_shape=tuple(outs), in_specs=[scalars(), whole(...  6.45 us
    pallas_call x1, Pallas kernels, prepare(): pl.pallas_call(prepare_kernel, out_shape=(head_major, head_major, head_ma...  4.17 us
    pallas_call x1, Pallas kernels, near_terms(): pl.pallas_call(near_terms_kernel, out_shape=shape((3, 384, FEAT), F32), i...  3.16 us
  transfers between devices with their start and end apart: 29, of which 10 were waited for; matrix products, arithmetic and copies ran while one was open for 0% of the time, Pallas kernels for 39%

commit v1 on v0

--- a/solution.py
+++ b/solution.py
@@ -616,8 +616,24 @@
     )(place, scores, qh, kh, vh, grad, keep, take, doc, docs, *earlier)
 
 
-def last_kernel(place, k_ref, v_ref, gq0, gk0, gv0, gq1, gk1, gv1, keep_ref, take_ref, doc_ref, docs_ref, *rest):
-    out_q, out_k, out_v, held_k, held_v = rest[-5:]
+def queries_kernel(low_ref, high_ref, *rest):
+    rest[-1][...] = jnp.swapaxes(jnp.concatenate([low_ref[...], high_ref[...]], 0), 0, 1)
+
+
+def queries_out(low, high, *earlier):
+    return pl.pallas_call(
+        queries_kernel,
+        out_shape=shape((TOK, HEADS, DIM), BF),
+        in_specs=[whole()] * 2 + [anywhere()] * len(earlier),
+        out_specs=whole(),
+        compiler_params=params(8),
+        cost_estimate=cost(TOK * FEAT, 2 * MIB),
+        name="queries_out",
+    )(low, high, *earlier)
+
+
+def last_kernel(place, k_ref, v_ref, gk0, gv0, gk1, gv1, keep_ref, take_ref, doc_ref, docs_ref, *rest):
+    out_k, out_v, held_k, held_v = rest[-4:]
     c = place[2]
     writes = (upright(docs_ref[...], DIM) == doc_ref[:1]).astype(F32)
     for h in range(HEADS):
@@ -625,7 +641,6 @@
         gk, gv = ((gk0, gv0), (gk1, gv1))[h // HALF]
         held_k[h] = (gk[h % HALF] + writes * dot(v_ref[h], state, 1, 1)).astype(BF)
         held_v[h] = (gv[h % HALF] + writes * dot(k_ref[h], state, 1, 0)).astype(BF)
-    out_q[...] = jnp.swapaxes(jnp.concatenate([gq0[...], gq1[...]], 0), 0, 1)
     out_k[...] = jnp.swapaxes(held_k[...], 0, 1)
     out_v[...] = jnp.swapaxes(held_v[...], 0, 1)
 
@@ -634,14 +649,14 @@
     out = shape((TOK, HEADS, DIM), BF)
     return pl.pallas_call(
         last_kernel,
-        out_shape=(out, out, out),
-        in_specs=[scalars()] + [whole()] * 12 + [anywhere()] * len(earlier),
-        out_specs=(whole(),) * 3,
+        out_shape=(out, out),
+        in_specs=[scalars()] + [whole()] * 10 + [anywhere()] * len(earlier),
+        out_specs=(whole(),) * 2,
         scratch_shapes=[pltpu.VMEM((HEADS, TOK, DIM), BF)] * 2,
         compiler_params=params(12),
         cost_estimate=cost(4 * HEADS * TOK * DIM * DIM, 9 * MIB),
         name="last",
-    )(place, kh, vh, *lower, *upper, keep, take, doc, docs, *earlier)
+    )(place, kh, vh, *lower[1:], *upper[1:], keep, take, doc, docs, *earlier)
 
 
 def pass_kernel(terms_ref, up_ref, down_ref, out_right, out_left):
@@ -815,7 +830,8 @@
     own, *shares = middle(terms, on, back_on)
     shares[1] = hold(shares[1], theirs)
     shares = [send(share, along_second(k)) for k, share in zip((1, 2, 3), shares)]
-    grad_queries, grad_keys, grad_values = last(
+    grad_queries = queries_out(lower[0], upper[0], theirs)
+    grad_keys, grad_values = last(
         place, kh, vh, lower, upper, back_mine, back_taken, back_doc, docs, own
     )
     layer_out = out_end(out_own, right, left, own)

time: 111 us -> 111 us (level)
    pallas_call x1 -> x2, Pallas kernels: 3.14 us -> 3.93 us  [the longest x1 2.8 us: last(): pl.pallas_call(last_kernel, out_shape=(out, out), in_specs=[scalars()] +...]
  transfers between devices with their start and end apart: 29 -> 29, of which waited for: 10 -> 9; matrix products, arithmetic and copies ran while one was open for 0% -> 0% of each run, Pallas kernels for 39% -> 40%
where the time goes in v1:
time: 111 us
  Pallas kernels  50.8 us (46%)
  starting transfers between devices  45.4 us (41%)
  waiting for transfers between devices  13.7 us (12%)
    ppermute x21, starting transfers between devices, send(): return lax.ppermute(array, 'seq', pairs)  32.2 us
    ppermute x21, waiting for transfers between devices, send(): return lax.ppermute(array, 'seq', pairs)  13.6 us
    ppermute x8, starting transfers between devices, along_head(): return lax.ppermute(array, 'head', [(i, (i + step) % 4) for i in range(4)])  13.2 us
    pallas_call x1, Pallas kernels, back(): pl.pallas_call(back_kernel, out_shape=(shape((HEADS, TOK, DIM), BF), half...  8.54 us
    pallas_call x2, Pallas kernels, inner(): pl.pallas_call(kernel, grid=(HALF // 2,), out_shape=(shape((HALF, TOK, DI...  7.69 us
    pallas_call x2, Pallas kernels, project(): pl.pallas_call(kernel, out_shape=tuple(outs), in_specs=[scalars(), whole(...  6.45 us
    pallas_call x1, Pallas kernels, prepare(): pl.pallas_call(prepare_kernel, out_shape=(head_major, head_major, head_ma...  4.17 us
    pallas_call x1, Pallas kernels, near_terms(): pl.pallas_call(near_terms_kernel, out_shape=shape((3, 384, FEAT), F32), i...  3.16 us
  transfers between devices with their start and end apart: 29, of which 9 were waited for; matrix products, arithmetic and copies ran while one was open for 0% of the time, Pallas kernels for 40%

profile of v1, /device:TPU:0, one launch (start us, length us, event | category | flops | bytes accessed | tf_op | source)
XLA Modules:
  0.0 111.0 jit_solution(4640043438554972735)
XLA Ops:
  0.8 4.2 %prepare.1 = (bf16[8,512,128]{2,1,0:T(8,128)(2,1)S(1)}, bf16[8,512,128]{2,1,0:T(8,128)(2,1)S(1)}, bf16[8,512,128]{2,1,0:T(8,128)(2,1)S(1)}, f32[520,128]{1,0:T(8...) custom-call(s32[4]{0:T(128)S(1)} %pad_add_fusion.place.refs_0_, bf16[512,8,128]{2,1,0:T(8,128)(2,1)} %q_hbm.1, ...), custom_call_target="tpu_custom_call" | custom-call | flops 134217728 | bytes 6291456 | tf_op jit(solution)/shard_map/prepare/pallas_call | solution.py:111
  4.9 1.6 %collective-permute-start.5 = (bf16[512,768]{1,0:T(8,128)(2,1)S(1)}, bf16[512,768]{1,0:T(8,128)(2,1)S(1)}, u32[]{:S(2)}, u32[]{:S(2)}) collective-permute-start(bf16[512,768]{1,0:T(8,128)(2,1)S(1)} %get-tuple-element.61.own_ref), channel_id=1, source_target_pairs={{0,1},{1,2},{2,3},{3,0},{4,5},{5,6},{6,7},{7,4},{8,9},{9,10},{10,1... | collective-permute-start | bytes 2359304 | tf_op jit(solution)/shard_map/ppermute | solution.py:780
  6.6 1.7 %collective-permute-start.6 = (bf16[512,768]{1,0:T(8,128)(2,1)S(1)}, bf16[512,768]{1,0:T(8,128)(2,1)S(1)}, u32[]{:S(2)}, u32[]{:S(2)}) collective-permute-start(bf16[512,768]{1,0:T(8,128)(2,1)S(1)} %get-tuple-element.61.own_ref), channel_id=1, source_target_pairs={{0,3},{1,0},{2,1},{3,2},{4,7},{5,4},{6,5},{7,6},{8,11},{9,8},{10,9... | collective-permute-start | bytes 2359304 | tf_op jit(solution)/shard_map/ppermute | solution.py:780
  8.2 1.5 %collective-permute-done.refs_2_ = f32[520,128]{1,0:T(8,128)S(1)} collective-permute-done((f32[520,128]{1,0:T(8,128)S(1)}, f32[520,128]{1,0:T(8,128)S(1)}, u32[]{:S(2)}, u32[]{:S(2)}) %collective-permute-start) | collective-permute-done | bytes 266272 | tf_op jit(solution)/shard_map/ppermute | solution.py:776
  10.4 2.1 %collective-permute-start.1 = (bf16[528,128]{1,0:T(8,128)(2,1)S(1)}, bf16[528,128]{1,0:T(8,128)(2,1)S(1)}, u32[]{:S(2)}, u32[]{:S(2)}) collective-permute-start(bf16[528,128]{1,0:T(8,128)(2,1)S(1)} %get-tuple-element.60.refs_1_), channel_id=1, source_target_pairs={{0,8},{4,12},{8,0},{12,4},{16,24},{20,28},{24,16},{28,20},{32,40},... | collective-permute-start | bytes 405512 | tf_op jit(solution)/shard_map/ppermute | solution.py:776
  12.5 1.4 %intra.2.refs_3_.intra0 = f32[4,512,128]{2,1,0:T(8,128)S(1)} custom-call(bf16[8,512,128]{2,1,0:T(8,128)(2,1)S(1)} %get-tuple-element.54.q_ref.refs_2_, bf16[8,512,128]{2,1,0:T(8,128)(2,1)S(1)} %get-tuple-element.55.k_ref.refs_3_, bf16[8,512,128]{2,1,0:T(8,128)(2,1)S(1)} %get-tuple-element.56.v_ref.refs_4_, s32[1,512]{1,0:T(1,128)S(1)} %bitcast.9, ...), custom_call_target="tpu_custom_call" | custom-call | flops 536870912 | bytes 3145728 | tf_op jit(solution)/shard_map/intra/pallas_call | solution.py:274
  13.9 2.4 %collective-permute-done.1.refs_2_ = bf16[528,128]{1,0:T(8,128)(2,1)S(1)} collective-permute-done((bf16[528,128]{1,0:T(8,128)(2,1)S(1)}, bf16[528,128]{1,0:T(8,128)(2,1)S(1)}, u32[]{:S(2)}, u32[]{:S(2)}) %collective-permute-start.1) | collective-permute-done | bytes 135200 | tf_op jit(solution)/shard_map/ppermute | solution.py:776
  17.0 3.8 %collective-permute-start.2 = (bf16[528,128]{1,0:T(8,128)(2,1)S(1)}, bf16[528,128]{1,0:T(8,128)(2,1)S(1)}, u32[]{:S(2)}, u32[]{:S(2)}) collective-permute-start(bf16[528,128]{1,0:T(8,128)(2,1)S(1)} %join.5.rest_0_.refs_1_), channel_id=1, source_target_pairs={{0,16},{4,20},{8,24},{12,28},{16,0},{20,4},{24,8},{28,12},{32,48},... | collective-permute-start | bytes 405512 | tf_op jit(solution)/shard_map/ppermute | solution.py:776
  20.7 1.0 upper_scores.1.refs_3_.refs_1_
  21.7 2.1 %collective-permute-done.2.refs_2_.refs_3_ = bf16[528,128]{1,0:T(8,128)(2,1)S(1)} collective-permute-done((bf16[528,128]{1,0:T(8,128)(2,1)S(1)}, bf16[528,128]{1,0:T(8,128)(2,1)S(1)}, u32[]{:S(2)}, u32[]{:S(2)}) %collective-permute-start.2) | collective-permute-done | bytes 135200 | tf_op jit(solution)/shard_map/ppermute | solution.py:776
  24.4 1.5 %intra.3.rest_0_.intra1 = f32[4,512,128]{2,1,0:T(8,128)S(1)} custom-call(bf16[8,512,128]{2,1,0:T(8,128)(2,1)S(1)} %get-tuple-element.54.q_ref.refs_2_, bf16[8,512,128]{2,1,0:T(8,128)(2,1)S(1)} %get-tuple-element.55.k_ref.refs_3_, bf16[8,512,128]{2,1,0:T(8,128)(2,1)S(1)} %get-tuple-element.56.v_ref.refs_4_, s32[1,512]{1,0:T(1,128)S(1)} %bitcast.11, ...), custom_call_target="tpu_custom_call" | custom-call | flops 536870912 | bytes 3145728 | tf_op jit(solution)/shard_map/intra/pallas_call | solution.py:274
  26.0 1.2 %collective-permute-start.8 = (bf16[256,768]{1,0:T(8,128)(2,1)S(1)}, bf16[256,768]{1,0:T(8,128)(2,1)S(1)}, u32[]{:S(2)}, u32[]{:S(2)}) collective-permute-start(bf16[256,768]{1,0:T(8,128)(2,1)S(1)} %get-tuple-element.62.refs_6_), channel_id=1, source_target_pairs={{0,1},{1,2},{2,3},{3,0},{4,5},{5,6},{6,7},{7,4},{8,9},{9,10},{10,1... | collective-permute-start | bytes 1179656 | tf_op jit(solution)/shard_map/ppermute | solution.py:780
  27.2 2.1 %collective-permute-start.9 = (bf16[256,768]{1,0:T(8,128)(2,1)S(1)}, bf16[256,768]{1,0:T(8,128)(2,1)S(1)}, u32[]{:S(2)}, u32[]{:S(2)}) collective-permute-start(bf16[256,768]{1,0:T(8,128)(2,1)S(1)} %get-tuple-element.67), channel_id=1, source_target_pairs={{0,3},{1,0},{2,1},{3,2},{4,7},{5,4},{6,5},{7,6},{8,11},{9,8},{10,9... | collective-permute-start | bytes 1179656 | tf_op jit(solution)/shard_map/ppermute | solution.py:780
  29.3 3.5 %collective-permute-start.3 = (bf16[528,128]{1,0:T(8,128)(2,1)S(1)}, bf16[528,128]{1,0:T(8,128)(2,1)S(1)}, u32[]{:S(2)}, u32[]{:S(2)}) collective-permute-start(bf16[528,128]{1,0:T(8,128)(2,1)S(1)} %join.6.rest_0_), channel_id=1, source_target_pairs={{0,32},{4,36},{8,40},{12,44},{16,48},{20,52},{24,56},{28,60},{32,6... | collective-permute-start | bytes 405512 | tf_op jit(solution)/shard_map/ppermute | solution.py:776
  32.7 4.8 %collective-permute-start.4 = (bf16[528,128]{1,0:T(8,128)(2,1)S(1)}, bf16[528,128]{1,0:T(8,128)(2,1)S(1)}, u32[]{:S(2)}, u32[]{:S(2)}) collective-permute-start(bf16[528,128]{1,0:T(8,128)(2,1)S(1)} %join.6.rest_0_), channel_id=1, source_target_pairs={{0,64},{4,68},{8,72},{12,76},{16,80},{20,84},{24,88},{28,92},{32,9... | collective-permute-start | bytes 405512 | tf_op jit(solution)/shard_map/ppermute | solution.py:776
  37.6 2.5 %collective-permute-done.4.refs_5_ = bf16[528,128]{1,0:T(8,128)(2,1)S(1)} collective-permute-done((bf16[528,128]{1,0:T(8,128)(2,1)S(1)}, bf16[528,128]{1,0:T(8,128)(2,1)S(1)}, u32[]{:S(2)}, u32[]{:S(2)}) %collective-permute-start.4) | collective-permute-done | bytes 135200 | tf_op jit(solution)/shard_map/ppermute | solution.py:776
  40.1 0.7 entry_state.2
  40.9 1.3 %collective-permute-done.7.take_ref.refs_7_ = bf16[512,128]{1,0:T(8,128)(2,1)S(1)} collective-permute-done((bf16[512,128]{1,0:T(8,128)(2,1)S(1)}, bf16[512,128]{1,0:T(8,128)(2,1)S(1)}, u32[]{:S(2)}, u32[]{:S(2)}) %collective-permute-start.7) | collective-permute-done | bytes 131104 | tf_op jit(solution)/shard_map/ppermute | solution.py:776
  42.3 1.5 %attend.1 = (f32[8,512,128]{2,1,0:T(8,128)S(1)}, bf16[512,1024]{1,0:T(8,128)(2,1)S(1)}) custom-call(s32[4]{0:T(128)S(1)} %pad_add_fusion.place.refs_0_, bf16[8,512,128]{2,1,0:T(8,128)(2,1)S(1)} %get-tuple-element.54.q_ref.refs_2_, f32[4,512,128]{2,1,0:T(8,128)S(1)} %intra.2.refs_3_.intra0, f32[4,512,128]{2,1,0:T(8,128)S(1)} %intra.3.rest_0_.intra1, ...), custom_call_target="tpu_custom_call" | custom-call | flops 134217728 | bytes 6291456 | tf_op jit(solution)/shard_map/attend/pallas_call | solution.py:329
  43.8 1.5 %turn.1 = (bf16[512,3072]{1,0:T(8,128)(2,1)S(1)}, bf16[4,4,96,512]{3,2,1,0:T(8,128)(2,1)S(1)}, bf16[4,4,96,512]{3,2,1,0:T(8,128)(2,1)S(1)}) custom-call(s32[4]{0:T(128)S(1)} %pad_add_fusion.place.refs_0_, bf16[512,768]{1,0:T(8,128)(2,1)S(1)} %get-tuple-element.61.own_ref, bf16[512,768]{1,0:T(8,128)(2,1)S(1)} %collective-permute-done.6.right_ref, ...), custom_call_target="tpu_custom_call" | custom-call | flops 1572864 | bytes 6291456 | tf_op jit(solution)/shard_map/turn/pallas_call | solution.py:465
  45.9 8.5 %back.1 = (bf16[8,512,128]{2,1,0:T(8,128)(2,1)S(1)}, f32[520,128]{1,0:T(8,128)S(1)}, f32[520,128]{1,0:T(8,128)S(1)}) custom-call(s32[4]{0:T(128)S(1)} %pad_add_fusion.place.refs_0_, bf16[512,3072]{1,0:T(8,128)(2,1)S(1)} %get-tuple-element.68.cot_ref, bf16[1024,3072]{1,0:T(8,128)(2,1)S(1)} %bitcast.7, f32[8,512,128]{2,1,0:T(8,128)S(1)} %get-tuple-element.69.attn_ref, ...), custom_call_target="tpu_custom_call" | custom-call | flops 3355443200 | bytes 15728640 | tf_op jit(solution)/shard_map/back/pallas_call | solution.py:505
  54.8 1.5 %far_terms.1 = (bf16[192,1024]{1,0:T(8,128)(2,1)S(1)}, bf16[192,1024]{1,0:T(8,128)(2,1)S(1)}) custom-call(s32[4]{0:T(128)S(1)} %pad_add_fusion.place.refs_0_, bf16[4,4,96,512]{3,2,1,0:T(8,128)(2,1)S(1)} %get-tuple-element.73.keep_ref, bf16[4,4,96,512]{3,2,1,0:T(8,128)(2,1)S(1)} %collective-permute-done.11.got_ref, ...), custom_call_target="tpu_custom_call" | custom-call | flops 805306368 | bytes 6291456 | tf_op jit(solution)/shard_map/far_terms/pallas_call | solution.py:538
  56.4 3.2 %collective-permute-start.20 = (bf16[192,1024]{1,0:T(8,128)(2,1)S(1)}, bf16[192,1024]{1,0:T(8,128)(2,1)S(1)}, u32[]{:S(2)}, u32[]{:S(2)}) collective-permute-start(bf16[192,1024]{1,0:T(8,128)(2,1)S(1)} %get-tuple-element.84), channel_id=1, source_target_pairs={{0,96},{4,28},{8,104},{12,4},{16,112},{20,12},{24,120},{28,20},{32... | collective-permute-start | bytes 1179656 | tf_op jit(solution)/shard_map/ppermute | solution.py:776
  59.6 0.6 chip_state.3
  60.2 1.7 %collective-permute-start.13 = (bf16[528,128]{1,0:T(8,128)(2,1)S(1)}, bf16[528,128]{1,0:T(8,128)(2,1)S(1)}, u32[]{:S(2)}, u32[]{:S(2)}) collective-permute-start(bf16[528,128]{1,0:T(8,128)(2,1)S(1)} %get-tuple-element.75.refs_1_), channel_id=1, source_target_pairs={{0,8},{4,12},{8,0},{12,4},{16,24},{20,28},{24,16},{28,20},{32,40},... | collective-permute-start | bytes 405512 | tf_op jit(solution)/shard_map/ppermute | solution.py:776
  61.9 1.8 %project.3 = (bf16[256,768]{1,0:T(8,128)(2,1)S(1)}, bf16[256,768]{1,0:T(8,128)(2,1)S(1)}) custom-call(s32[4]{0:T(128)S(1)} %pad_add_fusion.place.refs_0_, bf16[512,1024]{1,0:T(8,128)(2,1)S(1)} %get-tuple-element.66.rest_0_.normed_ref.refs_1_, bf16[1024,3072]{1,0:T(8,128)(2,1)S(1)} %bitcast.7, f32[520,128]{1,0:T(8,128)S(1)} %get-tuple-element.76.rest_0_.refs_3_.refs_1_), custom_call_target="tpu_custom_call" | custom-call | flops 805306368 | bytes 3145728 | tf_op jit(solution)/shard_map/project/pallas_call | solution.py:372
  64.0 3.0 %collective-permute-start.15 = (bf16[256,768]{1,0:T(8,128)(2,1)S(1)}, bf16[256,768]{1,0:T(8,128)(2,1)S(1)}, u32[]{:S(2)}, u32[]{:S(2)}) collective-permute-start(bf16[256,768]{1,0:T(8,128)(2,1)S(1)} %get-tuple-element.81), channel_id=1, source_target_pairs={{0,3},{1,0},{2,1},{3,2},{4,7},{5,4},{6,5},{7,6},{8,11},{9,8},{10,9... | collective-permute-start | bytes 1179656 | tf_op jit(solution)/shard_map/ppermute | solution.py:780
  67.0 3.2 %near_terms.1.refs_3_.terms_ref.own_ref = f32[3,384,1024]{2,1,0:T(8,128)S(1)} custom-call(s32[4]{0:T(128)S(1)} %pad_add_fusion.place.refs_0_, bf16[4,4,96,512]{3,2,1,0:T(8,128)(2,1)S(1)} %get-tuple-element.73.keep_ref, bf16[4,4,96,512]{3,2,1,0:T(8,128)(2,1)S(1)} %collective-permute-done.11.got_ref, ...), custom_call_target="tpu_custom_call" | custom-call | flops 2415919104 | bytes 10485760 | tf_op jit(solution)/shard_map/near_terms/pallas_call | solution.py:558
  70.8 3.7 %collective-permute-start.16 = (bf16[528,128]{1,0:T(8,128)(2,1)S(1)}, bf16[528,128]{1,0:T(8,128)(2,1)S(1)}, u32[]{:S(2)}, u32[]{:S(2)}) collective-permute-start(bf16[528,128]{1,0:T(8,128)(2,1)S(1)} %join.7.refs_3_.refs_1_), channel_id=1, source_target_pairs={{0,16},{4,20},{8,24},{12,28},{16,0},{20,4},{24,8},{28,12},{32,48},... | collective-permute-start | bytes 405512 | tf_op jit(solution)/shard_map/ppermute | solution.py:776
  74.6 0.8 collective-permute-start.21
  75.4 2.6 %collective-permute-start.22 = (bf16[384,1024]{1,0:T(8,128)(2,1)S(1)}, bf16[384,1024]{1,0:T(8,128)(2,1)S(1)}, u32[]{:S(2)}, u32[]{:S(2)}) collective-permute-start(bf16[384,1024]{1,0:T(8,128)(2,1)S(1)} %get-tuple-element.86), channel_id=1, source_target_pairs={{0,96},{4,28},{8,104},{12,4},{16,112},{20,12},{24,120},{28,20},{32... | collective-permute-start | bytes 2359304 | tf_op jit(solution)/shard_map/ppermute | solution.py:776
  77.9 4.7 %project.2 = (bf16[512,768]{1,0:T(8,128)(2,1)S(1)}, bf16[512,768]{1,0:T(8,128)(2,1)S(1)}, f32[512,768]{1,0:T(8,128)S(1)}) custom-call(s32[4]{0:T(128)S(1)} %pad_add_fusion.place.refs_0_, bf16[512,1024]{1,0:T(8,128)(2,1)S(1)} %get-tuple-element.66.rest_0_.normed_ref.refs_1_, bf16[1024,3072]{1,0:T(8,128)(2,1)S(1)} %bitcast.7, ...), custom_call_target="tpu_custom_call" | custom-call | flops 2415919104 | bytes 9437184 | tf_op jit(solution)/shard_map/project/pallas_call | solution.py:372
  82.7 0.6 join.8.rest_0_.refs_10_.refs_1_
  83.6 3.2 %collective-permute-start.18 = (bf16[512,768]{1,0:T(8,128)(2,1)S(1)}, bf16[512,768]{1,0:T(8,128)(2,1)S(1)}, u32[]{:S(2)}, u32[]{:S(2)}) collective-permute-start(bf16[512,768]{1,0:T(8,128)(2,1)S(1)} %get-tuple-element.83), channel_id=1, source_target_pairs={{0,3},{1,0},{2,1},{3,2},{4,7},{5,4},{6,5},{7,6},{8,11},{9,8},{10,9... | collective-permute-start | bytes 2359304 | tf_op jit(solution)/shard_map/ppermute | solution.py:780
  86.8 3.8 %inner.2 = (bf16[4,512,128]{2,1,0:T(8,128)(2,1)S(1)}, f32[4,512,128]{2,1,0:T(8,128)S(1)}, f32[4,512,128]{2,1,0:T(8,128)S(1)}) custom-call(s32[4]{0:T(128)S(1)} %pad_add_fusion.place.refs_0_, bf16[8,512,512]{2,1,0:T(8,128)(2,1)S(1)} %upper_scores.1.refs_3_.refs_1_, bf16[8,512,128]{2,1,0:T(8,128)(2,1)S(1)} %get-tuple-element.54.q_ref.refs_2_, ...), custom_call_target="tpu_custom_call" | custom-call | flops 1342177280 | bytes 5242880 | tf_op jit(solution)/shard_map/inner/pallas_call | solution.py:602
  90.7 1.2 %collective-permute-done.23.refs_2_.refs_4_ = bf16[528,128]{1,0:T(8,128)(2,1)S(1)} collective-permute-done((bf16[528,128]{1,0:T(8,128)(2,1)S(1)}, bf16[528,128]{1,0:T(8,128)(2,1)S(1)}, u32[]{:S(2)}, u32[]{:S(2)}) %collective-permute-start.23) | collective-permute-done | bytes 135200 | tf_op jit(solution)/shard_map/ppermute | solution.py:776
  91.8 0.6 join.9.refs_10_
  92.5 1.6 %collective-permute-start.24 = (bf16[528,128]{1,0:T(8,128)(2,1)S(1)}, bf16[528,128]{1,0:T(8,128)(2,1)S(1)}, u32[]{:S(2)}, u32[]{:S(2)}) collective-permute-start(bf16[528,128]{1,0:T(8,128)(2,1)S(1)} %join.9.refs_10_), channel_id=1, source_target_pairs={{0,64},{4,68},{8,72},{12,76},{16,80},{20,84},{24,88},{28,92},{32,9... | collective-permute-start | bytes 405512 | tf_op jit(solution)/shard_map/ppermute | solution.py:776
  94.1 3.8 %inner.3 = (bf16[4,512,128]{2,1,0:T(8,128)(2,1)S(1)}, f32[4,512,128]{2,1,0:T(8,128)S(1)}, f32[4,512,128]{2,1,0:T(8,128)S(1)}) custom-call(s32[4]{0:T(128)S(1)} %pad_add_fusion.place.refs_0_, bf16[8,512,512]{2,1,0:T(8,128)(2,1)S(1)} %upper_scores.1.refs_3_.refs_1_, bf16[8,512,128]{2,1,0:T(8,128)(2,1)S(1)} %get-tuple-element.54.q_ref.refs_2_, ...), custom_call_target="tpu_custom_call" | custom-call | flops 1342177280 | bytes 5242880 | tf_op jit(solution)/shard_map/inner/pallas_call | solution.py:602
  97.9 1.1 %collective-permute-done.24.refs_5_ = bf16[528,128]{1,0:T(8,128)(2,1)S(1)} collective-permute-done((bf16[528,128]{1,0:T(8,128)(2,1)S(1)}, bf16[528,128]{1,0:T(8,128)(2,1)S(1)}, u32[]{:S(2)}, u32[]{:S(2)}) %collective-permute-start.24) | collective-permute-done | bytes 135200 | tf_op jit(solution)/shard_map/ppermute | solution.py:776
  99.0 0.8 entry_state.3
  100.2 1.0 collective-permute-start.27
  101.2 2.3 %collective-permute-start.28 = (bf16[96,1024]{1,0:T(8,128)(2,1)S(1)}, bf16[96,1024]{1,0:T(8,128)(2,1)S(1)}, u32[]{:S(2)}, u32[]{:S(2)}) collective-permute-start(bf16[96,1024]{1,0:T(8,128)(2,1)S(1)} %get-tuple-element.102), channel_id=1, source_target_pairs={{0,24},{4,100},{8,0},{12,108},{16,8},{20,116},{24,16},{28,124},{32... | collective-permute-start | bytes 589832 | tf_op jit(solution)/shard_map/ppermute | solution.py:776
  103.6 1.1 %queries_out.1 = bf16[512,8,128]{2,1,0:T(8,128)(2,1)} custom-call(bf16[4,512,128]{2,1,0:T(8,128)(2,1)S(1)} %get-tuple-element.89.refs_3_.low_ref, bf16[4,512,128]{2,1,0:T(8,128)(2,1)S(1)} %get-tuple-element.90.refs_6_.high_ref, bf16[512,128]{1,0:T(8,128)(2,1)S(1)} %get-tuple-element.91.rest_0_), custom_call_target="tpu_custom_call" | custom-call | flops 524288 | bytes 2097152 | tf_op jit(solution)/shard_map/queries_out/pallas_call | solution.py:624
  104.7 1.2 %out_end.1 = bf16[512,768]{1,0:T(8,128)(2,1)} custom-call(f32[512,768]{1,0:T(8,128)S(1)} %get-tuple-element.77.own_ref, bf16[512,768]{1,0:T(8,128)(2,1)S(1)} %collective-permute-done.17.left_ref, bf16[512,768]{1,0:T(8,128)(2,1)S(1)} %collective-permute-done.18.right_ref, f32[96,1024]{1,0:T(8,128)S(1)} %get-tuple-element.87.rest_0_.own_ref), custom_call_target="tpu_custom_call" | custom-call | flops 786432 | bytes 4194304 | tf_op jit(solution)/shard_map/out_end/pallas_call | solution.py:432
  105.9 2.8 %last.1 = (bf16[512,8,128]{2,1,0:T(8,128)(2,1)}, bf16[512,8,128]{2,1,0:T(8,128)(2,1)}) custom-call(s32[4]{0:T(128)S(1)} %pad_add_fusion.place.refs_0_, bf16[8,512,128]{2,1,0:T(8,128)(2,1)S(1)} %get-tuple-element.55.k_ref.refs_3_, bf16[8,512,128]{2,1,0:T(8,128)(2,1)S(1)} %get-tuple-element.56.v_ref.refs_4_, f32[4,512,128]{2,1,0:T(8,128)S(1)} %get-tuple-element.92.gk0, ...), custom_call_target="tpu_custom_call" | custom-call | flops 268435456 | bytes 9437184 | tf_op jit(solution)/shard_map/last/pallas_call | solution.py:650
  109.1 1.0 collective-permute-done.28.p3
  110.1 0.8 end.1
  (49 shorter events, 5.4 us)
Async XLA Ops:
  0.7 11.7 %copy-start = (s32[512]{0:T(512)S(1)}, s32[512]{0:T(512)}, u32[]{:S(2)}) copy-start(s32[512]{0:T(512)} %param.9) | copy-start | bytes 6148
  4.9 20.9 %collective-permute-start.5 = (bf16[512,768]{1,0:T(8,128)(2,1)S(1)}, bf16[512,768]{1,0:T(8,128)(2,1)S(1)}, u32[]{:S(2)}, u32[]{:S(2)}) collective-permute-start(bf16[512,768]{1,0:T(8,128)(2,1)S(1)} %get-tuple-element.61.own_ref), channel_id=1, source_target_pairs={{0,1},{1,2},{2,3},{3,0},{4,5},{5,6},{6,7},{7,4},{8,9},{9,10},{10,1... | collective-permute-start | bytes 2359304 | tf_op jit(solution)/shard_map/ppermute | solution.py:780
  6.6 19.3 %collective-permute-start.6 = (bf16[512,768]{1,0:T(8,128)(2,1)S(1)}, bf16[512,768]{1,0:T(8,128)(2,1)S(1)}, u32[]{:S(2)}, u32[]{:S(2)}) collective-permute-start(bf16[512,768]{1,0:T(8,128)(2,1)S(1)} %get-tuple-element.61.own_ref), channel_id=1, source_target_pairs={{0,3},{1,0},{2,1},{3,2},{4,7},{5,4},{6,5},{7,6},{8,11},{9,8},{10,9... | collective-permute-start | bytes 2359304 | tf_op jit(solution)/shard_map/ppermute | solution.py:780
  8.2 1.5 %collective-permute-start = (f32[520,128]{1,0:T(8,128)S(1)}, f32[520,128]{1,0:T(8,128)S(1)}, u32[]{:S(2)}, u32[]{:S(2)}) collective-permute-start(f32[520,128]{1,0:T(8,128)S(1)} %get-tuple-element.58), channel_id=1, source_target_pairs={{0,4},{4,0},{8,12},{12,8},{16,20},{20,16},{24,28},{28,24},{32,36},... | collective-permute-start | bytes 798728 | tf_op jit(solution)/shard_map/ppermute | solution.py:776
  10.4 6.0 %collective-permute-start.1 = (bf16[528,128]{1,0:T(8,128)(2,1)S(1)}, bf16[528,128]{1,0:T(8,128)(2,1)S(1)}, u32[]{:S(2)}, u32[]{:S(2)}) collective-permute-start(bf16[528,128]{1,0:T(8,128)(2,1)S(1)} %get-tuple-element.60.refs_1_), channel_id=1, source_target_pairs={{0,8},{4,12},{8,0},{12,4},{16,24},{20,28},{24,16},{28,20},{32,40},... | collective-permute-start | bytes 405512 | tf_op jit(solution)/shard_map/ppermute | solution.py:776
  17.0 6.8 %collective-permute-start.2 = (bf16[528,128]{1,0:T(8,128)(2,1)S(1)}, bf16[528,128]{1,0:T(8,128)(2,1)S(1)}, u32[]{:S(2)}, u32[]{:S(2)}) collective-permute-start(bf16[528,128]{1,0:T(8,128)(2,1)S(1)} %join.5.rest_0_.refs_1_), channel_id=1, source_target_pairs={{0,16},{4,20},{8,24},{12,28},{16,0},{20,4},{24,8},{28,12},{32,48},... | collective-permute-start | bytes 405512 | tf_op jit(solution)/shard_map/ppermute | solution.py:776
  25.9 20.0 %slice-start = ((s8[6291456]{0:T(1024)(128)(4,1)}), s8[4194304]{0:T(1024)(128)(4,1)S(1)}, s32[]{:S(2)}) async-start(s8[6291456]{0:T(1024)(128)(4,1)} %bitcast.6), calls=%async_computation | async-start | bytes 8388608
  26.0 17.8 %collective-permute-start.8 = (bf16[256,768]{1,0:T(8,128)(2,1)S(1)}, bf16[256,768]{1,0:T(8,128)(2,1)S(1)}, u32[]{:S(2)}, u32[]{:S(2)}) collective-permute-start(bf16[256,768]{1,0:T(8,128)(2,1)S(1)} %get-tuple-element.62.refs_6_), channel_id=1, source_target_pairs={{0,1},{1,2},{2,3},{3,0},{4,5},{5,6},{6,7},{7,4},{8,9},{9,10},{10,1... | collective-permute-start | bytes 1179656 | tf_op jit(solution)/shard_map/ppermute | solution.py:780
  27.2 16.6 %collective-permute-start.9 = (bf16[256,768]{1,0:T(8,128)(2,1)S(1)}, bf16[256,768]{1,0:T(8,128)(2,1)S(1)}, u32[]{:S(2)}, u32[]{:S(2)}) collective-permute-start(bf16[256,768]{1,0:T(8,128)(2,1)S(1)} %get-tuple-element.67), channel_id=1, source_target_pairs={{0,3},{1,0},{2,1},{3,2},{4,7},{5,4},{6,5},{7,6},{8,11},{9,8},{10,9... | collective-permute-start | bytes 1179656 | tf_op jit(solution)/shard_map/ppermute | solution.py:780
  29.3 8.3 %collective-permute-start.3 = (bf16[528,128]{1,0:T(8,128)(2,1)S(1)}, bf16[528,128]{1,0:T(8,128)(2,1)S(1)}, u32[]{:S(2)}, u32[]{:S(2)}) collective-permute-start(bf16[528,128]{1,0:T(8,128)(2,1)S(1)} %join.6.rest_0_), channel_id=1, source_target_pairs={{0,32},{4,36},{8,40},{12,44},{16,48},{20,52},{24,56},{28,60},{32,6... | collective-permute-start | bytes 405512 | tf_op jit(solution)/shard_map/ppermute | solution.py:776
  32.7 7.3 %collective-permute-start.4 = (bf16[528,128]{1,0:T(8,128)(2,1)S(1)}, bf16[528,128]{1,0:T(8,128)(2,1)S(1)}, u32[]{:S(2)}, u32[]{:S(2)}) collective-permute-start(bf16[528,128]{1,0:T(8,128)(2,1)S(1)} %join.6.rest_0_), channel_id=1, source_target_pairs={{0,64},{4,68},{8,72},{12,76},{16,80},{20,84},{24,88},{28,92},{32,9... | collective-permute-start | bytes 405512 | tf_op jit(solution)/shard_map/ppermute | solution.py:776
  40.8 1.4 %collective-permute-start.7 = (bf16[512,128]{1,0:T(8,128)(2,1)S(1)}, bf16[512,128]{1,0:T(8,128)(2,1)S(1)}, u32[]{:S(2)}, u32[]{:S(2)}) collective-permute-start(bf16[512,128]{1,0:T(8,128)(2,1)S(1)} %get-tuple-element.64), channel_id=1, source_target_pairs={{0,4},{4,0},{8,12},{12,8},{16,20},{20,16},{24,28},{28,24},{32,36},... | collective-permute-start | bytes 393224 | tf_op jit(solution)/shard_map/ppermute | solution.py:776
  42.3 3.6 %slice-start.1 = ((s8[6291456]{0:T(1024)(128)(4,1)}), s8[2097152]{0:T(1024)(128)(4,1)S(1)}, s32[]{:S(2)}) async-start(s8[6291456]{0:T(1024)(128)(4,1)} %bitcast.6), calls=%async_computation.1 | async-start | bytes 4194304
  45.3 9.5 %collective-permute-start.11 = (bf16[4,4,96,512]{3,2,1,0:T(8,128)(2,1)S(1)}, bf16[4,4,96,512]{3,2,1,0:T(8,128)(2,1)S(1)}, u32[]{:S(2)}, u32[]{:S(2)}) collective-permute-start(bf16[4,4,96,512]{3,2,1,0:T(8,128)(2,1)S(1)} %get-tuple-element.70.rest_0_), channel_id=1, source_target_pairs={{0,4},{4,0},{8,12},{12,8},{16,20},{20,16},{24,28},{28,24},{32,36},... | collective-permute-start | bytes 4718600 | tf_op jit(solution)/shard_map/ppermute | solution.py:776
  45.5 9.3 %collective-permute-start.12 = (bf16[512,1024]{1,0:T(8,128)(2,1)S(1)}, bf16[512,1024]{1,0:T(8,128)(2,1)S(1)}, u32[]{:S(2)}, u32[]{:S(2)}) collective-permute-start(bf16[512,1024]{1,0:T(8,128)(2,1)S(1)} %get-tuple-element.66.rest_0_.normed_ref.refs_1_), channel_id=1, source_target_pairs={{0,4},{4,0},{8,12},{12,8},{16,20},{20,16},{24,28},{28,24},{32,36},... | collective-permute-start | bytes 3145736 | tf_op jit(solution)/shard_map/ppermute | solution.py:776
  54.4 5.2 %collective-permute-start.10 = (f32[520,128]{1,0:T(8,128)S(1)}, f32[520,128]{1,0:T(8,128)S(1)}, u32[]{:S(2)}, u32[]{:S(2)}) collective-permute-start(f32[520,128]{1,0:T(8,128)S(1)} %get-tuple-element.72), channel_id=1, source_target_pairs={{0,4},{4,0},{8,12},{12,8},{16,20},{20,16},{24,28},{28,24},{32,36},... | collective-permute-start | bytes 798728 | tf_op jit(solution)/shard_map/ppermute | solution.py:776
  56.3 18.1 %collective-permute-start.19 = (bf16[192,1024]{1,0:T(8,128)(2,1)S(1)}, bf16[192,1024]{1,0:T(8,128)(2,1)S(1)}, u32[]{:S(2)}, u32[]{:S(2)}) collective-permute-start(bf16[192,1024]{1,0:T(8,128)(2,1)S(1)} %get-tuple-element.74.refs_3_), channel_id=1, source_target_pairs={{0,32},{4,12},{8,40},{12,20},{16,48},{20,28},{24,56},{28,4},{32,64... | collective-permute-start | bytes 1179656 | tf_op jit(solution)/shard_map/ppermute | solution.py:776
  56.4 18.0 %collective-permute-start.20 = (bf16[192,1024]{1,0:T(8,128)(2,1)S(1)}, bf16[192,1024]{1,0:T(8,128)(2,1)S(1)}, u32[]{:S(2)}, u32[]{:S(2)}) collective-permute-start(bf16[192,1024]{1,0:T(8,128)(2,1)S(1)} %get-tuple-element.84), channel_id=1, source_target_pairs={{0,96},{4,28},{8,104},{12,4},{16,112},{20,12},{24,120},{28,20},{32... | collective-permute-start | bytes 1179656 | tf_op jit(solution)/shard_map/ppermute | solution.py:776
  60.2 9.9 %collective-permute-start.13 = (bf16[528,128]{1,0:T(8,128)(2,1)S(1)}, bf16[528,128]{1,0:T(8,128)(2,1)S(1)}, u32[]{:S(2)}, u32[]{:S(2)}) collective-permute-start(bf16[528,128]{1,0:T(8,128)(2,1)S(1)} %get-tuple-element.75.refs_1_), channel_id=1, source_target_pairs={{0,8},{4,12},{8,0},{12,4},{16,24},{20,28},{24,16},{28,20},{32,40},... | collective-permute-start | bytes 405512 | tf_op jit(solution)/shard_map/ppermute | solution.py:776
  63.7 19.6 %collective-permute-start.14 = (bf16[256,768]{1,0:T(8,128)(2,1)S(1)}, bf16[256,768]{1,0:T(8,128)(2,1)S(1)}, u32[]{:S(2)}, u32[]{:S(2)}) collective-permute-start(bf16[256,768]{1,0:T(8,128)(2,1)S(1)} %get-tuple-element.80), channel_id=1, source_target_pairs={{0,1},{1,2},{2,3},{3,0},{4,5},{5,6},{6,7},{7,4},{8,9},{9,10},{10,1... | collective-permute-start | bytes 1179656 | tf_op jit(solution)/shard_map/ppermute | solution.py:780
  64.0 19.3 %collective-permute-start.15 = (bf16[256,768]{1,0:T(8,128)(2,1)S(1)}, bf16[256,768]{1,0:T(8,128)(2,1)S(1)}, u32[]{:S(2)}, u32[]{:S(2)}) collective-permute-start(bf16[256,768]{1,0:T(8,128)(2,1)S(1)} %get-tuple-element.81), channel_id=1, source_target_pairs={{0,3},{1,0},{2,1},{3,2},{4,7},{5,4},{6,5},{7,6},{8,11},{9,8},{10,9... | collective-permute-start | bytes 1179656 | tf_op jit(solution)/shard_map/ppermute | solution.py:780
  70.8 11.9 %collective-permute-start.16 = (bf16[528,128]{1,0:T(8,128)(2,1)S(1)}, bf16[528,128]{1,0:T(8,128)(2,1)S(1)}, u32[]{:S(2)}, u32[]{:S(2)}) collective-permute-start(bf16[528,128]{1,0:T(8,128)(2,1)S(1)} %join.7.refs_3_.refs_1_), channel_id=1, source_target_pairs={{0,16},{4,20},{8,24},{12,28},{16,0},{20,4},{24,8},{28,12},{32,48},... | collective-permute-start | bytes 405512 | tf_op jit(solution)/shard_map/ppermute | solution.py:776
  74.6 25.2 %collective-permute-start.21 = (bf16[384,1024]{1,0:T(8,128)(2,1)S(1)}, bf16[384,1024]{1,0:T(8,128)(2,1)S(1)}, u32[]{:S(2)}, u32[]{:S(2)}) collective-permute-start(bf16[384,1024]{1,0:T(8,128)(2,1)S(1)} %get-tuple-element.85), channel_id=1, source_target_pairs={{0,32},{4,12},{8,40},{12,20},{16,48},{20,28},{24,56},{28,4},{32,64... | collective-permute-start | bytes 2359304 | tf_op jit(solution)/shard_map/ppermute | solution.py:776
  75.4 24.4 %collective-permute-start.22 = (bf16[384,1024]{1,0:T(8,128)(2,1)S(1)}, bf16[384,1024]{1,0:T(8,128)(2,1)S(1)}, u32[]{:S(2)}, u32[]{:S(2)}) collective-permute-start(bf16[384,1024]{1,0:T(8,128)(2,1)S(1)} %get-tuple-element.86), channel_id=1, source_target_pairs={{0,96},{4,28},{8,104},{12,4},{16,112},{20,12},{24,120},{28,20},{32... | collective-permute-start | bytes 2359304 | tf_op jit(solution)/shard_map/ppermute | solution.py:776
  83.5 20.0 %collective-permute-start.17 = (bf16[512,768]{1,0:T(8,128)(2,1)S(1)}, bf16[512,768]{1,0:T(8,128)(2,1)S(1)}, u32[]{:S(2)}, u32[]{:S(2)}) collective-permute-start(bf16[512,768]{1,0:T(8,128)(2,1)S(1)} %get-tuple-element.82), channel_id=1, source_target_pairs={{0,1},{1,2},{2,3},{3,0},{4,5},{5,6},{6,7},{7,4},{8,9},{9,10},{10,1... | collective-permute-start | bytes 2359304 | tf_op jit(solution)/shard_map/ppermute | solution.py:780
  83.6 21.1 %collective-permute-start.18 = (bf16[512,768]{1,0:T(8,128)(2,1)S(1)}, bf16[512,768]{1,0:T(8,128)(2,1)S(1)}, u32[]{:S(2)}, u32[]{:S(2)}) collective-permute-start(bf16[512,768]{1,0:T(8,128)(2,1)S(1)} %get-tuple-element.83), channel_id=1, source_target_pairs={{0,3},{1,0},{2,1},{3,2},{4,7},{5,4},{6,5},{7,6},{8,11},{9,8},{10,9... | collective-permute-start | bytes 2359304 | tf_op jit(solution)/shard_map/ppermute | solution.py:780
  86.8 5.0 %collective-permute-start.23 = (bf16[528,128]{1,0:T(8,128)(2,1)S(1)}, bf16[528,128]{1,0:T(8,128)(2,1)S(1)}, u32[]{:S(2)}, u32[]{:S(2)}) collective-permute-start(bf16[528,128]{1,0:T(8,128)(2,1)S(1)} %join.8.rest_0_.refs_10_.refs_1_), channel_id=1, source_target_pairs={{0,32},{4,36},{8,40},{12,44},{16,48},{20,52},{24,56},{28,60},{32,0... | collective-permute-start | bytes 405512 | tf_op jit(solution)/shard_map/ppermute | solution.py:776
  92.5 6.6 %collective-permute-start.24 = (bf16[528,128]{1,0:T(8,128)(2,1)S(1)}, bf16[528,128]{1,0:T(8,128)(2,1)S(1)}, u32[]{:S(2)}, u32[]{:S(2)}) collective-permute-start(bf16[528,128]{1,0:T(8,128)(2,1)S(1)} %join.9.refs_10_), channel_id=1, source_target_pairs={{0,64},{4,68},{8,72},{12,76},{16,80},{20,84},{24,88},{28,92},{32,9... | collective-permute-start | bytes 405512 | tf_op jit(solution)/shard_map/ppermute | solution.py:776
  100.1 9.1 %collective-permute-start.26 = (bf16[96,1024]{1,0:T(8,128)(2,1)S(1)}, bf16[96,1024]{1,0:T(8,128)(2,1)S(1)}, u32[]{:S(2)}, u32[]{:S(2)}) collective-permute-start(bf16[96,1024]{1,0:T(8,128)(2,1)S(1)} %get-tuple-element.100), channel_id=1, source_target_pairs={{0,8},{4,36},{8,16},{12,44},{16,24},{20,52},{24,0},{28,60},{32,40}... | collective-permute-start | bytes 589832 | tf_op jit(solution)/shard_map/ppermute | solution.py:776
  100.2 9.0 %collective-permute-start.27 = (bf16[96,1024]{1,0:T(8,128)(2,1)S(1)}, bf16[96,1024]{1,0:T(8,128)(2,1)S(1)}, u32[]{:S(2)}, u32[]{:S(2)}) collective-permute-start(bf16[96,1024]{1,0:T(8,128)(2,1)S(1)} %hold.1), channel_id=1, source_target_pairs={{0,16},{4,68},{8,24},{12,76},{16,0},{20,84},{24,8},{28,92},{32,48}... | collective-permute-start | bytes 589832 | tf_op jit(solution)/shard_map/ppermute | solution.py:776
  101.2 8.9 %collective-permute-start.28 = (bf16[96,1024]{1,0:T(8,128)(2,1)S(1)}, bf16[96,1024]{1,0:T(8,128)(2,1)S(1)}, u32[]{:S(2)}, u32[]{:S(2)}) collective-permute-start(bf16[96,1024]{1,0:T(8,128)(2,1)S(1)} %get-tuple-element.102), channel_id=1, source_target_pairs={{0,24},{4,100},{8,0},{12,108},{16,8},{20,116},{24,16},{28,124},{32... | collective-permute-start | bytes 589832 | tf_op jit(solution)/shard_map/ppermute | solution.py:776
  103.6 2.3 %collective-permute-start.25 = (bf16[512,128]{1,0:T(8,128)(2,1)S(1)}, bf16[512,128]{1,0:T(8,128)(2,1)S(1)}, u32[]{:S(2)}, u32[]{:S(2)}) collective-permute-start(bf16[512,128]{1,0:T(8,128)(2,1)S(1)} %get-tuple-element.91.rest_0_), channel_id=1, source_target_pairs={{0,4},{4,0},{8,12},{12,8},{16,20},{20,16},{24,28},{28,24},{32,36},... | collective-permute-start | bytes 393224 | tf_op jit(solution)/shard_map/ppermute | solution.py:776
